TPU v7x, 256 devices: a whole 4x4x8 slice. The times are simulated.
256 devices in a mesh: px: 8 (over z), py: 32 (over y, x, core).
Axes of the slice: x: 4, y: 4, z: 8, core: 2. Of those that a mesh axis runs over, the one named last changes fastest.
Arguments:
- current_state: float32 [5, 125, 262144], P(None, None, ('px', 'py')), may hold values from -6 to 6
- state_old: float32 [5, 125, 262144], P(None, None, ('px', 'py')), may hold values from -6 to 6
- jacobian: float32 [262144], P(('px', 'py')), may hold values from 0.5 to 2
- volume_operator_list: float32 [3, 125, 125], replicated, may hold values from -0.3125 to 0.3125
- flux_jacobian_list: float32 [3, 5, 5], replicated, may hold values from -2.5 to 2.5
- penalty: float32 [5], replicated, may hold values from 0.5 to 2
- cut_owner: int32 [10240, 1], P(('px', 'py')), may hold values from 0 to 31; in each aligned block of 40 rows (0 to 39, 40 to 79, ...) at most 2 rows name the same one
- cut_element: int32 [10240], P(('px', 'py')), may hold values from 0 to 1023
- cut_mass: float32 [10240, 125, 125], P(('px', 'py')), may hold values from -0.5 to 0.5
- cut_operator: float32 [10240, 125, 125], P(('px', 'py')), may hold values from -0.5 to 0.5
- body_holder_index: int32 [48], P('px'), may hold values from 0 to 31
- body_points: float32 [1536, 3, 128], P(('px', 'py')), may hold values from -1 to 1
- body_normals: float32 [1536, 3, 128], P(('px', 'py')), may hold values from -6 to 6
- body_weights: float32 [1536, 128], P(('px', 'py')), may hold values from 0.01 to 0.1
- covered: int32 [1536, 16], P(('px', 'py')), may hold values from 0 to 1023
Outputs:
- residual: float32 [5, 125, 262144], P(None, None, ('px', 'py'))
Inputs may be any that keep to these rules, and one draw needn't show every extreme that they name: `cut_owner`: among the 40 rows of one device no owner is named by more than 2 rows, a bound that some block reaches. Owners are py indices within the same slab. `cut_element`: several cut blocks may belong to one element; their terms add. `body_holder_index`: only the slot of the owning device is read for each body. `covered`: an element may be listed more than once; its terms add.
All inputs are finite; a program needn't handle non-finite values.
Results may differ from a plain program's by a relative error of at most 0.0001.
Values sent between devices are 32-bit elements; how exact they have to be, the bound alone decides.
A program may use at most 128 MiB of HBM per device.

v0:
```python
import jax
import jax.numpy as jnp
from jax import lax
from jax.sharding import PartitionSpec as P

DEGREE = 4
LAYERS = 8
BODIES = 6


TOP_PRECISION = lax.Precision.HIGHEST


def from_behind(value, axis, steps):
    count = lax.axis_size(axis)
    leading, last = (max(0, -steps), min(count, count - steps))
    return lax.ppermute(value, axis, [(source, source + steps) for source in range(leading, last)])


def broadcast(value, axis, source):
    kept = jnp.where(lax.axis_index(axis) == source, value, 0).astype(value.dtype)
    return lax.psum(kept, axis)


def mode_weights():
    degree_one = DEGREE + 1
    mode_index = jnp.arange(degree_one**3, dtype=jnp.int32)
    degree_x = (mode_index // (degree_one * degree_one)).astype(jnp.float32)
    degree_y = (mode_index // degree_one % degree_one).astype(jnp.float32)
    degree_z = (mode_index % degree_one).astype(jnp.float32)
    return 8.0 / ((2.0 * degree_x + 1.0) * (2.0 * degree_y + 1.0) * (2.0 * degree_z + 1.0))


def legendre_table(coords):
    poly_table = [jnp.ones_like(coords), coords]
    for degree_now in range(1, DEGREE):
        poly_table.append(
            (
                (2.0 * degree_now + 1.0) * coords * poly_table[degree_now]
                - degree_now * poly_table[degree_now - 1]
            )
            / (degree_now + 1.0)
        )
    return jnp.stack(poly_table[: DEGREE + 1], axis=0)


def basis_rows(points):
    along_x = legendre_table(points[..., 0, :])
    along_y = legendre_table(points[..., 1, :])
    along_z = legendre_table(points[..., 2, :])
    basis_vals = along_x[:, None, None] * along_y[None, :, None] * along_z[None, None, :]
    leading = points.shape[:-2]
    basis_vals = basis_vals.reshape(((DEGREE + 1) ** 3,) + leading + (points.shape[-1],))
    return jnp.moveaxis(basis_vals, 0, -2)


def slot_table(slot_index, slot_total):
    return (slot_index[:, None] == jnp.arange(slot_total, dtype=jnp.int32)[None, :]).astype(
        jnp.float32
    )


def pick_rows(flat_field, elem_ids):
    selector = (
        elem_ids[:, None] == jnp.arange(flat_field.shape[1], dtype=jnp.int32)[None, :]
    ).astype(jnp.float32)
    return lax.dot_general(selector, flat_field, (((1,), (1,)), ((), ())), precision=TOP_PRECISION)


def pick_columns(flat_field, elem_ids):
    selector = (
        jnp.arange(flat_field.shape[1], dtype=jnp.int32)[:, None] == elem_ids[None, :]
    ).astype(jnp.float32)
    return jnp.dot(flat_field, selector, precision=TOP_PRECISION)


def add_columns(flat_field, terms, elem_ids, term_dim):
    selector = (
        elem_ids[:, None] == jnp.arange(flat_field.shape[1], dtype=jnp.int32)[None, :]
    ).astype(jnp.float32)
    return flat_field + lax.dot_general(
        terms, selector, (((term_dim,), (0,)), ((), ())), precision=TOP_PRECISION
    )


def local(
    current_state,
    state_old,
    jacobian,
    volume_operator_list,
    flux_jacobian_list,
    penalty,
    cut_owner,
    cut_element,
    cut_mass,
    cut_operator,
    body_holder_index,
    body_points,
    body_normals,
    body_weights,
    covered,
):
    degree_one = DEGREE + 1
    face_count = degree_one * degree_one
    nvar = current_state.shape[0]
    mode_count = current_state.shape[1]
    elem_count = current_state.shape[2]
    column_count = elem_count // LAYERS
    flat_width = nvar * mode_count
    split_modes = current_state.reshape(nvar, degree_one, face_count, elem_count)
    parity = jnp.where(jnp.arange(degree_one, dtype=jnp.int32) % 2 == 0, 1.0, -1.0).astype(
        jnp.float32
    )
    upper_trace = jnp.sum(split_modes, axis=1).reshape(nvar, face_count, LAYERS, column_count)
    lower_trace = jnp.sum(split_modes * parity[None, :, None, None], axis=1).reshape(
        nvar, face_count, LAYERS, column_count
    )
    above_rim = from_behind(lower_trace[:, :, 0, :], "px", -1)
    below_rim = from_behind(upper_trace[:, :, LAYERS - 1, :], "px", 1)
    change = current_state - state_old
    residual = mode_weights()[None, :, None] * jacobian[None, None, :] * change
    for space_direction in range(3):
        blended_state = jnp.einsum(
            "jr,rti->jti",
            flux_jacobian_list[space_direction],
            current_state,
            precision=TOP_PRECISION,
        )
        residual = residual - jnp.einsum(
            "fz,jzx->jfx",
            volume_operator_list[space_direction],
            blended_state,
            precision=TOP_PRECISION,
        )
    from_above = jnp.concatenate([lower_trace[:, :, 1:, :], above_rim[:, :, None, :]], axis=2)
    from_below = jnp.concatenate([below_rim[:, :, None, :], upper_trace[:, :, :-1, :]], axis=2)
    jump_top = (from_above - upper_trace).reshape(nvar, face_count, elem_count)
    jump_bottom = (from_below - lower_trace).reshape(nvar, face_count, elem_count)
    face_term = penalty[:, None, None, None] * (
        jump_top[:, None] + parity[None, :, None, None] * jump_bottom[:, None]
    )
    residual = residual - face_term.reshape(nvar, mode_count, elem_count)
    flat_state = current_state.reshape(flat_width, elem_count)
    flat_change = change.reshape(flat_width, elem_count)
    flat_residual = residual.reshape(flat_width, elem_count)
    peer_count = lax.axis_size("py")
    cut_count = cut_owner.shape[0]
    capacity = max(2, cut_count * 3 // (2 * peer_count) + 1)
    slot_total = peer_count * capacity
    destination = cut_owner[:, 0]
    peer_ids = jnp.arange(peer_count, dtype=jnp.int32)
    onehot_dest = (destination[:, None] == peer_ids[None, :]).astype(jnp.int32)
    before = jnp.cumsum(onehot_dest, axis=0) - onehot_dest
    position = jnp.sum(before * onehot_dest, axis=1)
    slot_index = destination * capacity + position
    placing = slot_table(slot_index, slot_total)
    packed_ids = lax.dot_general(
        placing,
        cut_element.astype(jnp.float32)[:, None],
        (((0,), (0,)), ((), ())),
        precision=TOP_PRECISION,
    ).reshape(peer_count, capacity)
    block_pairs = jnp.stack([cut_mass, cut_operator], axis=1).reshape(
        cut_count, 2 * mode_count * mode_count
    )
    packed = lax.dot_general(
        placing, block_pairs, (((0,), (0,)), ((), ())), precision=TOP_PRECISION
    )
    packed = packed.reshape(peer_count, capacity, 2, mode_count, mode_count)
    pairs_in = lax.all_to_all(packed, "py", split_axis=0, concat_axis=0, tiled=True)
    ids_in = lax.all_to_all(packed_ids, "py", split_axis=0, concat_axis=0, tiled=True)
    slot_elem = ids_in.reshape(-1).astype(jnp.int32)
    flat_pairs = pairs_in.reshape(-1, 2, mode_count, mode_count)
    change_rows = pick_rows(flat_change, slot_elem).reshape(-1, nvar, mode_count)
    state_rows = pick_rows(flat_state, slot_elem).reshape(-1, nvar, mode_count)
    local_terms = jnp.einsum(
        "smn,svn->svm", flat_pairs[:, 0], change_rows, precision=TOP_PRECISION
    ) - jnp.einsum("smn,svn->svm", flat_pairs[:, 1], state_rows, precision=TOP_PRECISION)
    cut_terms = local_terms.reshape(ids_in.shape + (nvar, mode_count))
    slot_elem = ids_in.reshape(-1).astype(jnp.int32)
    flat_residual = add_columns(flat_residual, cut_terms.reshape(-1, flat_width), slot_elem, 0)
    covered_count = covered.shape[1]
    all_targets = covered.reshape(-1)
    gathered_all = pick_columns(flat_state, all_targets).reshape(
        nvar, mode_count, BODIES, covered_count
    )
    lifted_parts = []
    for body_index in range(BODIES):
        owner_id = body_holder_index[body_index]
        own_basis = basis_rows(body_points[body_index])
        basis_now, normals, weights = (
            broadcast(own_basis, "py", owner_id),
            broadcast(body_normals[body_index], "py", owner_id),
            broadcast(body_weights[body_index], "py", owner_id),
        )
        gathered = gathered_all[:, :, body_index, :]
        surf_trace = jnp.einsum("mq,vmo->vqo", basis_now, gathered, precision=TOP_PRECISION)
        normal_x = normals[0][:, None]
        normal_y = normals[1][:, None]
        normal_z = normals[2][:, None]
        speed = normal_x * surf_trace[1] + normal_y * surf_trace[2] + normal_z * surf_trace[3]
        body_wall_flux = jnp.stack(
            [
                speed + 0.5 * surf_trace[0],
                normal_x * surf_trace[4],
                normal_y * surf_trace[4],
                normal_z * surf_trace[4],
                1.4 * speed,
            ],
            axis=0,
        )
        weighted = body_wall_flux * weights[None, :, None]
        lifted_parts.append(jnp.einsum("mq,vqo->vmo", basis_now, weighted, precision=TOP_PRECISION))
    all_lifted = jnp.stack(lifted_parts, axis=2).reshape(flat_width, BODIES * covered_count)
    flat_residual = add_columns(flat_residual, -all_lifted, all_targets, 1)
    return flat_residual.reshape(nvar, mode_count, elem_count)


def solution(mesh):
    in_specs = (
        P(None, None, ("px", "py")),
        P(None, None, ("px", "py")),
        P(("px", "py")),
        P(),
        P(),
        P(),
        P(("px", "py"), None),
        P(("px", "py")),
        P(("px", "py"), None, None),
        P(("px", "py"), None, None),
        P("px"),
        P(("px", "py"), None, None),
        P(("px", "py"), None, None),
        P(("px", "py"), None),
        P(("px", "py"), None),
    )
    out_specs = P(None, None, ("px", "py"))
    return jax.shard_map(local, mesh=mesh, in_specs=in_specs, out_specs=out_specs, check_vma=False)
```

profile of v0, /device:TPU:1, one launch (start us, length us, event | category | flops | bytes accessed | tf_op | source)
XLA Modules:
  0.0 288.4 jit_solution(15736663644584482716)
XLA Ops:
  6.5 3.8 %reshape.2372 = f32[5,5,25,1024]{3,2,1,0:T(8,128)} reshape(f32[5,125,1024]{2,1,0:T(8,128)} %param.15) | data formatting | bytes 5120000 | tf_op jit(solution)/shard_map/reshape | solution.py:110
  10.3 3.5 %fusion.136 = (f32[5,25,1024]{2,1,0:T(8,128)}, f32[5,25,1024]{2,1,0:T(8,128)S(1)}) fusion(f32[5,5,25,1024]{3,2,1,0:T(8,128)} %reshape.2372, f32[5]{0:T(128)S(1)} %compare_select_fusion), kind=kLoop, calls=%fused_computation.373 | loop fusion | flops 1664000 | bytes 3584020 | tf_op jit(solution)/shard_map/reduce_sum | solution.py:114
  17.8 2.0 reshape.2374
  21.6 5.6 %collective-permute-start.1 = (f32[5,25,128]{2,1,0:T(8,128)}, f32[5,25,128]{2,1,0:T(8,128)}, u32[]{:S(2)}, u32[]{:S(2)}) collective-permute-start(f32[5,25,128]{2,1,0:T(8,128)} %bitcast.422), channel_id=1, source_target_pairs={{0,32},{32,64},{64,96},{96,128},{128,160},{160,192},{192,224},{1,3... | collective-permute-start | bytes 192008 | tf_op jit(solution)/shard_map/ppermute | solution.py:17
  28.5 8.1 %all-to-all-start = ((f32[32,1,2]{2,1,0:T(1,128)}), f32[32,1,2]{2,1,0:T(1,128)S(1)}, u32[]{:S(2)}, u32[]{:S(2)}) async-start(f32[32,1,2]{2,1,0:T(1,128)} %copy.83), calls=%async_computation | async-start | bytes 32768 | tf_op jit(solution)/shard_map/all_to_all | solution.py:171
  57.7 5.5 %fusion.3 = f32[5,125,1024]{2,0,1:T(8,128)S(1)} fusion(f32[5,125,1024]{2,1,0:T(8,128)S(1)} %copy-done, f32[1,5,5]{2,0,1:T(1,128)S(1)} %get-tuple-element.155), kind=kOutput, calls=%fused_computation.4 | convolution fusion | flops 38400000 | bytes 5120100 | tf_op jit(solution)/shard_map/jr,rti->jti/dot_general | solution.py:123
  63.2 5.5 %fusion.5 = f32[5,125,1024]{2,0,1:T(8,128)S(1)} fusion(f32[5,125,1024]{2,1,0:T(8,128)S(1)} %copy-done, f32[1,5,5]{2,0,1:T(1,128)S(1)} %get-tuple-element.154), kind=kOutput, calls=%fused_computation.6 | convolution fusion | flops 38400000 | bytes 5120100 | tf_op jit(solution)/shard_map/jr,rti->jti/dot_general | solution.py:123
  68.8 6.1 %fusion.12 = f32[5,1024,125]{1,2,0:T(8,128)} fusion(f32[5,125,1024]{2,0,1:T(8,128)S(1)} %fusion.3, f32[3,125,125]{2,1,0:T(8,128)S(1)} %copy-done.7), kind=kOutput, calls=%fused_computation.19 | convolution fusion | flops 960000000 | bytes 6721536 | tf_op jit(solution)/shard_map/fz,jzx->jfx/dot_general | solution.py:129
  74.9 5.8 %fusion.14 = f32[5,1024,125]{1,2,0:T(8,128)} fusion(f32[5,125,1024]{2,0,1:T(8,128)S(1)} %fusion.5, f32[3,125,125]{2,1,0:T(8,128)S(1)} %copy-done.7), kind=kOutput, calls=%fused_computation.21 | convolution fusion | flops 960000000 | bytes 6721536 | tf_op jit(solution)/shard_map/fz,jzx->jfx/dot_general | solution.py:129
  80.7 6.9 %fusion.7 = f32[5,125,1024]{2,0,1:T(8,128)} fusion(f32[5,125,1024]{2,1,0:T(8,128)S(1)} %copy-done, f32[1,5,5]{2,0,1:T(1,128)S(1)} %get-tuple-element.153), kind=kOutput, calls=%fused_computation.8 | convolution fusion | flops 38400000 | bytes 5120100 | tf_op jit(solution)/shard_map/jr,rti->jti/dot_general | solution.py:123
  88.0 3.3 %copy.84 = f32[40,2,125,125]{3,2,1,0:T(8,128)} copy(f32[40,2,125,125]{3,0,2,1:T(8,128)S(1)} %pad_maximum_fusion) | data formatting | bytes 10000000 | tf_op jit(solution)/shard_map/stack | solution.py:163
  91.2 6.2 %reshape.2376 = f32[40,31250]{1,0:T(8,128)} reshape(f32[40,2,125,125]{3,2,1,0:T(8,128)} %copy.84) | data formatting | bytes 10000000 | tf_op jit(solution)/shard_map/reshape | solution.py:163
  97.5 8.5 %dot_general.96 = f32[2,125,125,40]{2,1,0,3:T(8,128)} reshape(f32[31250,40]{0,1:T(8,128)} %bitcast.427) | data formatting | bytes 10000000 | tf_op jit(solution)/shard_map/dot_general | solution.py:166
  106.0 12.5 %fusion = f32[32,2,2,125,125]{4,0,3,2,1:T(8,128)} fusion(f32[2,125,125,40]{2,1,0,3:T(8,128)} %dot_general.96, s32[32,2]{0,1:T(2,128)S(1)} %multiply_add_fusion, s32[40]{0:T(128)S(1)} %fusion.135), kind=kOutput, calls=%fused_computation.1 | convolution fusion | flops 960002560 | bytes 13000416 | tf_op jit(solution)/shard_map/dot_general | solution.py:166
  118.6 3.2 %convolution_bitcast_fusion = f32[625,96]{0,1:T(8,128)S(1)} fusion(f32[625,1024]{1,0:T(8,128)} %reshape.2378, s32[96]{0:T(128)S(1)} %eq.164), kind=kOutput, calls=%fused_computation.27 | convolution fusion | flops 737476608 | bytes 2800384 | tf_op jit(solution)/shard_map/dot_general | solution.py:74
  127.4 13.0 %copy.86 = f32[32,2,2,125,125]{4,2,3,1,0:T(2,128)} copy(f32[32,2,2,125,125]{4,0,3,2,1:T(8,128)} %fusion) | data formatting | bytes 16000000 | tf_op jit(solution)/shard_map/dot_general | solution.py:166
  140.4 7.4 %all-to-all-start.1 = ((f32[32,2,2,125,125]{4,2,3,1,0:T(2,128)}), f32[32,2,2,125,125]{4,2,3,1,0:T(2,128)}, u32[]{:S(2)}, u32[]{:S(2)}) async-start(f32[32,2,2,125,125]{4,2,3,1,0:T(2,128)} %copy.86), calls=%async_computation.1 | async-start | bytes 16384000 | tf_op jit(solution)/shard_map/all_to_all | solution.py:170
  148.0 3.3 %fusion.21 = f32[64,5,125]{2,0,1:T(8,128)S(1)} fusion(f32[5,125,1024]{2,1,0:T(8,128)S(1)} %copy-done, f32[5,125,1024]{2,1,0:T(8,128)} %param.16, s32[64]{0:T(128)S(1)} %convert_element_type.71), kind=kOutput, calls=%fused_computation.28 | convolution fusion | flops 492225536 | bytes 5280256 | tf_op jit(solution)/shard_map/dot_general | solution.py:67
  151.4 2.2 fusion.36
  158.7 2.1 add.500
  160.9 4.0 %add.501 = f32[5,125,1024]{2,1,0:T(8,128)} reshape(f32[5,5,25,1024]{3,2,1,0:T(8,128)} %add.500) | data formatting | bytes 5120000 | tf_op jit(solution)/shard_map/add | solution.py:140
  165.8 2.0 pad_maximum_fusion.2
  170.9 2.1 mul.2670
  173.0 4.2 %mul.2671 = f32[5,125,1024]{2,1,0:T(8,128)} reshape(f32[5,5,25,1024]{3,2,1,0:T(8,128)} %mul.2670) | data formatting | bytes 5120000 | tf_op jit(solution)/shard_map/mul | solution.py:140
  177.3 13.4 %fusion.11 = f32[5,125,1024]{2,1,0:T(8,128)} fusion(f32[5,1024,125]{1,2,0:T(8,128)} %fusion.12, f32[5,1024,125]{1,2,0:T(8,128)} %fusion.14, f32[5,125,1024]{2,1,0:T(8,128)} %add.501, f32[5,125,1024]{2,1,0:T(8,128)} %mul.2671, f32[5,125,1024]{2,0,1:T(8,128)} %fusion.7, f32[125]{0:T(128)S(1)} %mul.2668, f32[5]{0:T(128)S(1)} %copy-done.21, ...), kind=kOutput, calls=%fused_computation.16 | convolution fusion | flops 965760000 | bytes 22901256 | tf_op jit(solution)/shard_map/fz,jzx->jfx/dot_general | solution.py:129
  190.7 2.1 reshape.2375
  192.8 44.1 %all-reduce.3.cloned.1.call-done = (f32[125,128]{1,0:T(8,128)}, f32[3,128]{1,0:T(4,128)}, f32[128]{0:T(128)}, f32[125,128]{1,0:T(8,128)}, f32[3,128]{1,0:T(4,128...) async-done(((f32[125,128]{1,0:T(8,128)}, f32[3,128]{1,0:T(4,128)}, ...) | async-done | bytes 396304 | tf_op jit(solution)/shard_map/psum | solution.py:22
  253.5 4.5 %copy.101 = f32[32,2,2,125,125]{4,3,1,0,2:T(8,128)S(1)} copy(f32[32,2,2,125,125]{4,2,3,1,0:T(2,128)} %all-to-all-done.1) | data formatting | bytes 16000000 | tf_op jit(solution)/shard_map/reshape | solution.py:173
  258.1 7.0 %fusion.9 = f32[64,5,125]{2,1,0:T(8,128)S(1)} fusion(f32[64,2,125,125]{3,2,0,1:T(8,128)S(1)} %bitcast.425, f32[64,5,125]{2,0,1:T(8,128)S(1)} %copy-done.5), kind=kOutput, calls=%fused_computation.11 | convolution fusion | flops 60000000 | bytes 4518144 | tf_op jit(solution)/shard_map/smn,svn->svm/dot_general | solution.py:178
  265.1 7.4 %fusion.20 = f32[64,5,125]{2,1,0:T(8,128)} fusion(f32[64,5,125]{2,1,0:T(8,128)S(1)} %fusion.9, f32[64,2,125,125]{3,2,0,1:T(8,128)S(1)} %bitcast.426, f32[64,5,125]{2,0,1:T(8,128)S(1)} %fusion.21), kind=kOutput, calls=%fused_computation.26 | convolution fusion | flops 60040000 | bytes 4780288 | tf_op jit(solution)/shard_map/smn,svn->svm/dot_general | solution.py:176
  274.9 3.0 %add_add_fusion = f32[625,1024]{1,0:T(8,128)} fusion(f32[625,1024]{1,0:T(8,128)S(1)} %reshape.2375, f32[625,1024]{1,0:T(8,128)S(1)} %fusion.34, f32[625,96]{0,1:T(8,128)S(1)} %copy-done.6, s32[96]{0:T(128)S(1)} %eq.164), kind=kOutput, calls=%fused_computation.25 | convolution fusion | flops 738658304 | bytes 7920384 | tf_op jit(solution)/shard_map/dot_general | solution.py:81
  277.9 3.5 %reshape.2380 = f32[5,125,1024]{2,1,0:T(8,128)} reshape(f32[625,1024]{1,0:T(8,128)} %add_add_fusion) | data formatting | bytes 5120000 | tf_op jit(solution)/shard_map/reshape | solution.py:216
  (179 shorter events, 58.2 us)
Async XLA Ops:
  10.3 16.9 %copy-start.20 = (s32[40,1]{0,1:T(1,128)S(1)}, s32[40,1]{0,1:T(1,128)}, u32[]{:S(2)}) copy-start(s32[40,1]{0,1:T(1,128)} %param.21) | copy-start | bytes 484
  13.8 13.8 %copy-start.22 = (s32[40]{0:T(128)S(1)}, s32[40]{0:T(128)}, u32[]{:S(2)}) copy-start(s32[40]{0:T(128)} %param.22) | copy-start | bytes 484
  13.8 23.2 %copy-start.13 = (f32[6,3,128]{2,1,0:T(4,128)S(1)}, f32[6,3,128]{2,1,0:T(4,128)}, u32[]{:S(2)}) copy-start(f32[6,3,128]{2,1,0:T(4,128)} %param.26) | copy-start | bytes 27652
  13.8 25.1 %copy-start.14 = (s32[6]{0:T(128)S(1)}, s32[6]{0:T(128)}, u32[]{:S(2)}) copy-start(s32[6]{0:T(128)} %param.25) | copy-start | bytes 76
  13.8 30.5 %copy-start.15 = (f32[6,3,128]{2,1,0:T(4,128)S(1)}, f32[6,3,128]{2,1,0:T(4,128)}, u32[]{:S(2)}) copy-start(f32[6,3,128]{2,1,0:T(4,128)} %param.27) | copy-start | bytes 27652
  13.8 31.2 %copy-start.19 = (f32[6,128]{1,0:T(8,128)S(1)}, f32[6,128]{1,0:T(8,128)}, u32[]{:S(2)}) copy-start(f32[6,128]{1,0:T(8,128)} %param.28) | copy-start | bytes 9220
  14.7 41.2 %copy-start = (f32[5,125,1024]{2,1,0:T(8,128)S(1)}, f32[5,125,1024]{2,1,0:T(8,128)}, u32[]{:S(2)}) copy-start(f32[5,125,1024]{2,1,0:T(8,128)} %param.15) | copy-start | bytes 7680004
  16.5 137.0 %collective-permute-start = (f32[5,25,128]{2,1,0:T(8,128)}, f32[5,25,128]{2,1,0:T(8,128)}, u32[]{:S(2)}, u32[]{:S(2)}) collective-permute-start(f32[5,25,128]{2,1,0:T(8,128)} %bitcast.423), channel_id=1, source_target_pairs={{32,0},{64,32},{96,64},{128,96},{160,128},{192,160},{224,192},{33,... | collective-permute-start | bytes 192008 | tf_op jit(solution)/shard_map/ppermute | solution.py:17
  21.6 143.3 %collective-permute-start.1 = (f32[5,25,128]{2,1,0:T(8,128)}, f32[5,25,128]{2,1,0:T(8,128)}, u32[]{:S(2)}, u32[]{:S(2)}) collective-permute-start(f32[5,25,128]{2,1,0:T(8,128)} %bitcast.422), channel_id=1, source_target_pairs={{0,32},{32,64},{64,96},{96,128},{128,160},{160,192},{192,224},{1,3... | collective-permute-start | bytes 192008 | tf_op jit(solution)/shard_map/ppermute | solution.py:17
  28.5 111.9 %all-to-all-start = ((f32[32,1,2]{2,1,0:T(1,128)}), f32[32,1,2]{2,1,0:T(1,128)S(1)}, u32[]{:S(2)}, u32[]{:S(2)}) async-start(f32[32,1,2]{2,1,0:T(1,128)} %copy.83), calls=%async_computation | async-start | bytes 32768 | tf_op jit(solution)/shard_map/all_to_all | solution.py:171
  36.6 200.3 %all-reduce.3.cloned.1.call-start = ((), (), s32[]{:S(2)}) async-start(), calls=%async_computation.2 | async-start | bytes 817152 | tf_op jit(solution)/shard_map/psum | solution.py:22
  55.9 1.9 copy-start.16
  63.2 5.5 %copy-start.7 = (f32[3,125,125]{2,1,0:T(8,128)S(1)}, f32[3,125,125]{2,1,0:T(8,128)}, u32[]{:S(2)}) copy-start(f32[3,125,125]{2,1,0:T(8,128)} %param.18) | copy-start | bytes 562504
  80.7 6.9 %copy-start.1 = (f32[40,125,125]{2,0,1:T(8,128)S(1)}, f32[40,125,125]{2,0,1:T(8,128)}, u32[]{:S(2)}) copy-start(f32[40,125,125]{2,0,1:T(8,128)} %param.24) | copy-start | bytes 7500004
  80.7 6.9 %copy-start.2 = (f32[40,125,125]{2,0,1:T(8,128)S(1)}, f32[40,125,125]{2,0,1:T(8,128)}, u32[]{:S(2)}) copy-start(f32[40,125,125]{2,0,1:T(8,128)} %param.23) | copy-start | bytes 7500004
  106.0 12.5 %copy-start.18 = (s32[6,16]{1,0:T(8,128)S(1)}, s32[6,16]{1,0:T(8,128)}, u32[]{:S(2)}) copy-start(s32[6,16]{1,0:T(8,128)} %param.29) | copy-start | bytes 1156
  118.5 4.2 %copy-start.17 = (f32[1024]{0:T(1024)S(1)}, f32[1024]{0:T(1024)}, u32[]{:S(2)}) copy-start(f32[1024]{0:T(1024)} %param.17) | copy-start | bytes 12292
  140.4 113.2 %all-to-all-start.1 = ((f32[32,2,2,125,125]{4,2,3,1,0:T(2,128)}), f32[32,2,2,125,125]{4,2,3,1,0:T(2,128)}, u32[]{:S(2)}, u32[]{:S(2)}) async-start(f32[32,2,2,125,125]{4,2,3,1,0:T(2,128)} %copy.86), calls=%async_computation.1 | async-start | bytes 16384000 | tf_op jit(solution)/shard_map/all_to_all | solution.py:170
  151.3 3.1 %copy-start.4 = (f32[5,25,7,128]{3,2,1,0:T(8,128)S(1)}, f32[5,25,7,128]{3,2,1,0:T(8,128)}, u32[]{:S(2)}) copy-start(f32[5,25,7,128]{3,2,1,0:T(8,128)} %slice.570) | copy-start | bytes 1344004
  173.0 4.2 %copy-start.3 = (f32[125,1024]{1,0:T(8,128)S(1)}, f32[125,1024]{1,0:T(8,128)}, u32[]{:S(2)}) copy-start(f32[125,1024]{1,0:T(8,128)} %broadcast_multiply_fusion) | copy-start | bytes 1536004
  173.0 4.2 %copy-start.21 = (f32[5]{0:T(128)S(1)}, f32[5]{0:T(128)}, u32[]{:S(2)}) copy-start(f32[5]{0:T(128)} %param.20) | copy-start | bytes 64
  190.7 46.3 %copy-start.12 = (f32[5,125,1,16]{1,0,3,2:T(8,128)S(1)}, f32[5,125,1,16]{1,0,3,2:T(8,128)}, u32[]{:S(2)}) copy-start(f32[5,125,1,16]{1,0,3,2:T(8,128)} %get-tuple-element.78) | copy-start | bytes 120004
  190.7 48.1 %copy-start.11 = (f32[5,125,1,16]{1,0,3,2:T(8,128)S(1)}, f32[5,125,1,16]{1,0,3,2:T(8,128)}, u32[]{:S(2)}) copy-start(f32[5,125,1,16]{1,0,3,2:T(8,128)} %get-tuple-element.77) | copy-start | bytes 120004
  190.7 50.9 %copy-start.10 = (f32[5,125,1,16]{1,0,3,2:T(8,128)S(1)}, f32[5,125,1,16]{1,0,3,2:T(8,128)}, u32[]{:S(2)}) copy-start(f32[5,125,1,16]{1,0,3,2:T(8,128)} %get-tuple-element.76) | copy-start | bytes 120004
  190.7 52.0 %copy-start.9 = (f32[5,125,1,16]{1,0,3,2:T(8,128)S(1)}, f32[5,125,1,16]{1,0,3,2:T(8,128)}, u32[]{:S(2)}) copy-start(f32[5,125,1,16]{1,0,3,2:T(8,128)} %get-tuple-element.75) | copy-start | bytes 120004
  190.7 53.1 %copy-start.8 = (f32[5,125,1,16]{1,0,3,2:T(8,128)S(1)}, f32[5,125,1,16]{1,0,3,2:T(8,128)}, u32[]{:S(2)}) copy-start(f32[5,125,1,16]{1,0,3,2:T(8,128)} %get-tuple-element.74) | copy-start | bytes 120004
  253.5 4.5 %copy-start.5 = (f32[64,5,125]{2,0,1:T(8,128)S(1)}, f32[64,5,125]{2,0,1:T(8,128)}, u32[]{:S(2)}) copy-start(f32[64,5,125]{2,0,1:T(8,128)} %fusion.36) | copy-start | bytes 480004
  272.5 2.4 copy-start.6
Sparse Core Ops, SparseCore 0:
  56.0 180.9 all-reduce.2
where the time goes:
time: 294 us; the launch traced here: 288 us
  matrix products  96 us (33%)
  local copies, waits for them, and re-layouts  93.8 us (32%)
  waiting for transfers between devices  44.1 us (15%)
  starting transfers between devices  22.8 us (8%)
  between operations  18.3 us (6%)
  other arithmetic  13.4 us (5%)
    psum x1, waiting for transfers between devices, broadcast(): return lax.psum(kept, axis)  44.1 us
    dot_general x3, matrix products, local(): jnp.einsum('fz,jzx->jfx', volume_operator_list[space_direction], blended_...  25.4 us
    dot_general x2, local copies, waits for them, and re-layouts, local(): lax.dot_general(placing, block_pairs, (((0,), (0,)), ((), ())), precision...  21.5 us
    dot_general x3, matrix products, local(): jnp.einsum('jr,rti->jti', flux_jacobian_list[space_direction], current_st...  17.9 us
    dot_general x1, matrix products, local(): lax.dot_general(placing, block_pairs, (((0,), (0,)), ((), ())), precision...  12.5 us
    all_to_all x1, starting transfers between devices, local(): lax.all_to_all(packed_ids, 'py', split_axis=0, concat_axis=0, tiled=True)  8.14 us
    all_to_all x1, starting transfers between devices, local(): lax.all_to_all(packed, 'py', split_axis=0, concat_axis=0, tiled=True)  7.43 us
    dot_general x1, matrix products, local(): jnp.einsum('smn,svn->svm', flat_pairs[:, 0], change_rows, precision=TOP_P...  7.37 us
  transfers between devices with their start and end apart: 5, of which 1 were waited for; matrix products, arithmetic and copies ran while one was open for 57% of the time, Pallas kernels for 0%

commit v1 on v0

v1 whole, which is shorter than its diff:
```python
import functools

import jax
import jax.numpy as jnp
from jax import lax
from jax.experimental import pallas as pl
from jax.experimental.pallas import tpu as pltpu
from jax.sharding import PartitionSpec as P

F32 = jnp.float32
BF16 = jnp.bfloat16
MESH = pl.DeviceIdType.MESH
NVAR = 5
MODES = 125
PAD = 128
ELEM = 1024
PEERS = 32
CUTS = 40
CPAD = 48
SLOTS = 64
BODIES = 6
COVER = 16
TERMS = SLOTS + BODIES * COVER
WIDTH = NVAR * PAD
MBLOCK = 16


def split(value):
    high = value.astype(BF16)
    low = (value - high.astype(F32)).astype(BF16)
    return high, low


def dot(left, right):
    return jnp.dot(left, right, preferred_element_type=F32)


def dot_nt(left, right):
    return lax.dot_general(left, right, (((1,), (1,)), ((), ())), preferred_element_type=F32)


def iota(shape, dim):
    return lax.broadcasted_iota(jnp.int32, shape, dim)


def divmod_const(index, by):
    exact = index.astype(F32)
    whole = jnp.floor((exact + 0.5) * (1.0 / by))
    return whole, exact - whole * by


def parity_of(whole):
    return 1.0 - 2.0 * (whole - 2.0 * jnp.floor(whole * 0.5))


def pad_rows(value):
    zero = jnp.zeros((PAD - value.shape[0], value.shape[1]), value.dtype)
    return jnp.concatenate([value, zero], axis=0)


def pad_lanes(value):
    zero = jnp.zeros((value.shape[0], PAD - value.shape[1]), value.dtype)
    return jnp.concatenate([value, zero], axis=1)


def to_column(row, rows, lanes):
    spread = jnp.broadcast_to(row, (rows, lanes))
    pick = iota((rows, lanes), 0) == iota((rows, lanes), 1)
    return jnp.sum(jnp.where(pick, spread, 0), axis=1, keepdims=True)


def kernel(
    state_hbm,
    old_hbm,
    mass_hbm,
    oper_hbm,
    jac,
    vol,
    flux,
    penalty,
    owner,
    elem,
    holder,
    points,
    normals,
    weights,
    covered,
    out_hbm,
    st,
    so,
    mats,
    uhl,
    chl,
    vpad,
    mhh,
    mlo,
    trx,
    part,
    cuth,
    cutl,
    ids_row,
    ids_all,
    onehot,
    p2send,
    p2recv,
    p3send,
    p3recv,
    gbody,
    xh,
    xl,
    tmode,
    bown,
    bgot1,
    bsum1,
    bgot2,
    bsum2,
    bgot3,
    basis,
    tbody,
    load_sem,
    out_sem,
    rim_send,
    rim_recv,
    id_send,
    id_recv,
    p2_send,
    p2_recv,
    p3_send,
    p3_recv,
    b_send,
    b_recv,
):
    me = lax.axis_index("py")
    pz = lax.axis_index("px")
    npx = lax.axis_size("px")

    load_state = pltpu.make_async_copy(state_hbm, st, load_sem.at[0])
    load_old = pltpu.make_async_copy(old_hbm, so, load_sem.at[1])
    load_mass = pltpu.make_async_copy(mass_hbm, mats.at[0], load_sem.at[2])
    load_oper = pltpu.make_async_copy(oper_hbm, mats.at[1], load_sem.at[3])
    load_state.start()
    load_old.start()
    load_mass.start()
    load_oper.start()

    barrier = pltpu.get_barrier_semaphore()
    above = lax.rem(pz + 1, npx)
    below = lax.rem(pz + npx - 1, npx)

    def greet(r, carry):
        pl.semaphore_signal(
            barrier, inc=1, device_id={"py": lax.rem(me + r, PEERS)}, device_id_type=MESH
        )
        return carry

    lax.fori_loop(1, PEERS, greet, 0)
    for neighbour in (above, below):
        pl.semaphore_signal(barrier, inc=1, device_id={"px": neighbour}, device_id_type=MESH)

    own_row = jnp.broadcast_to(owner[...], (CUTS, CUTS))
    own_col = to_column(owner[...], CUTS, CUTS)
    elem_col = to_column(elem[...], CUTS, CUTS)
    same = own_row == own_col
    row_c, lane_c = iota((CUTS, CUTS), 0), iota((CUTS, CUTS), 1)
    pos_col = jnp.sum(jnp.where(same & (lane_c < row_c), 1, 0), axis=1, keepdims=True)
    pos_row = jnp.sum(jnp.where(same & (row_c < lane_c), 1, 0), axis=0, keepdims=True)
    slot_col = pos_col * PEERS + own_col
    slot_row = pos_row * PEERS + owner[...]
    placed = jnp.where(slot_col == iota((CUTS, PAD), 1), elem_col + 1, 0)
    ids_row[...] = jnp.sum(placed, axis=0, keepdims=True) - 1

    bown[...] = jnp.zeros_like(bown)
    body_row = iota((BODIES, 128), 0)
    held = jnp.zeros((BODIES, 128), jnp.int32)
    for b in range(BODIES):
        held = jnp.where(body_row == b, jnp.where(holder[b] == me, 1, 0), held)
    held = held == 1
    for d in range(3):
        bown[d, 0:BODIES, :] = jnp.where(held, points[:, d, :], 0.0)
        bown[3 + d, 0:BODIES, :] = jnp.where(held, normals[:, d, :], 0.0)
    bown[6, 0:BODIES, :] = jnp.where(held, weights[...], 0.0)

    pl.semaphore_wait(barrier, PEERS + 1)

    def id_copy(r):
        return pltpu.make_async_remote_copy(
            src_ref=ids_row,
            dst_ref=ids_all.at[pl.ds(me, 1), :],
            send_sem=id_send.at[r],
            recv_sem=id_recv,
            device_id={"py": lax.rem(me + r, PEERS)},
            device_id_type=MESH,
        )

    def id_start(r, carry):
        id_copy(r).start()
        return carry

    lax.fori_loop(1, PEERS, id_start, 0)
    pltpu.make_async_copy(ids_row, ids_all.at[pl.ds(me, 1), :], id_recv).start()

    core = lax.rem(me, 2)
    px_in = lax.rem(me // 2, 4)
    py_in = me // 8
    sibling = me + 1 - 2 * core
    body1 = pltpu.make_async_remote_copy(
        src_ref=bown,
        dst_ref=bgot1,
        send_sem=b_send.at[0],
        recv_sem=b_recv.at[0],
        device_id={"py": sibling},
        device_id_type=MESH,
    )
    body1.start()

    vpad[...] = jnp.zeros_like(vpad)
    for d in range(3):
        vpad[d, 0:MODES, 0:MODES] = vol[d]
    ri, rf = divmod_const(iota((PAD, PAD), 0), 25)
    ci, cf = divmod_const(iota((PAD, PAD), 1), 25)
    inside = (ri < 5.0) & (ci < 5.0)
    own_face = jnp.where(inside & (rf == cf), 1.0 + parity_of(ri) * parity_of(ci), 0.0)

    def build(v, carry):
        rows = pl.ds(pl.multiple_of(v * PAD, PAD), PAD)
        for w in range(NVAR):
            block = jnp.where(v == w, penalty[v], 0.0) * own_face
            for d in range(3):
                block = block - flux[v, d, w] * vpad[d]
            high, low = split(block)
            mhh[rows, w * PAD : (w + 1) * PAD] = high
            mhh[rows, WIDTH + w * PAD : WIDTH + (w + 1) * PAD] = high
            mlo[rows, w * PAD : (w + 1) * PAD] = low
        return carry

    lax.fori_loop(0, NVAR, build, 0)

    ti, tf = divmod_const(iota((64, PAD), 1), 25)
    tr_row = iota((64, PAD), 0)
    tr_lower = tr_row >= 32
    tr_f = jnp.where(tr_lower, tr_row - 32, tr_row).astype(F32)
    trace_op = jnp.where(
        (tf == tr_f) & (ti < 5.0), jnp.where(tr_lower, parity_of(ti), 1.0), 0.0
    ).astype(BF16)
    l64 = lax.rem(iota((PAD, PAD), 1), 64)
    l32 = lax.rem(iota((PAD, PAD), 1), 32)
    expand_op = jnp.where(
        (rf == l32.astype(F32)) & (ri < 5.0), jnp.where(l64 < 32, parity_of(ri), 1.0), 0.0
    ).astype(BF16)

    load_state.wait()
    load_old.wait()

    def split_state(j, carry):
        cols = pl.ds(pl.multiple_of(j * 256, 256), 256)
        tcols = pl.ds(pl.multiple_of(j * 256 + 128, 128), 256)
        for v in range(NVAR):
            rows = pl.ds(v * PAD, PAD)
            u = st[v, :, cols]
            high, low = split(pad_rows(u))
            uhl[0, rows, cols] = high
            uhl[1, rows, cols] = low
            trx[v, :, tcols] = dot(trace_op, high) + dot(trace_op, low)
            high, low = split(pad_rows(u - so[v, :, cols]))
            chl[0, rows, cols] = high
            chl[1, rows, cols] = low
        return carry

    lax.fori_loop(0, 4, split_state, 0)

    rim_down = pltpu.make_async_remote_copy(
        src_ref=trx.at[:, 32:64, 128:256],
        dst_ref=trx.at[:, 32:64, 1152:1280],
        send_sem=rim_send.at[0],
        recv_sem=rim_recv.at[0],
        device_id={"px": below},
        device_id_type=MESH,
    )
    rim_up = pltpu.make_async_remote_copy(
        src_ref=trx.at[:, 0:32, 1024:1152],
        dst_ref=trx.at[:, 0:32, 0:128],
        send_sem=rim_send.at[1],
        recv_sem=rim_recv.at[1],
        device_id={"px": above},
        device_id_type=MESH,
    )
    rim_down.start()
    rim_up.start()

    body1.wait_recv()
    bsum1[...] = bown[...] + bgot1[...]
    body2 = []
    for r in range(1, 4):
        body2.append(
            pltpu.make_async_remote_copy(
                src_ref=bsum1,
                dst_ref=bgot2.at[r - 1],
                send_sem=b_send.at[r],
                recv_sem=b_recv.at[r],
                device_id={"py": py_in * 8 + lax.rem(px_in + r, 4) * 2 + core},
                device_id_type=MESH,
            )
        )
        body2[-1].start()

    pltpu.make_async_copy(ids_all, ids_all, id_recv).wait()
    asked = ids_all[...]
    lane = iota((PEERS, 128), 1)
    elem_lane = iota((PEERS, ELEM), 1)
    for k in range(2):
        wanted = jnp.sum(jnp.where(lane == me + k * PEERS, asked, 0), axis=1, keepdims=True)
        onehot[k * PEERS : (k + 1) * PEERS, :] = jnp.where(wanted == elem_lane, 1.0, 0.0).astype(BF16)
    cover_lane = iota((COVER, ELEM), 1)
    for b in range(BODIES):
        wanted = to_column(covered[b : b + 1, :], COVER, COVER)
        start = SLOTS + b * COVER
        onehot[start : start + COVER, :] = jnp.where(wanted == cover_lane, 1.0, 0.0).astype(BF16)

    state_high = dot_nt(onehot[...], uhl[0])
    state_low = dot_nt(onehot[...], uhl[1])
    state_cols = state_high + state_low
    change_cols = dot_nt(onehot[0:SLOTS, :], chl[0]) + dot_nt(onehot[0:SLOTS, :], chl[1])
    for k in range(2):
        rows = slice(k * PEERS, (k + 1) * PEERS)
        for v in range(NVAR):
            lanes = slice(v * PAD, (v + 1) * PAD)
            p2send[k * 10 + v] = change_cols[rows, lanes]
            p2send[k * 10 + 5 + v] = state_cols[rows, lanes]
    for v in range(NVAR):
        gbody[v] = state_cols[SLOTS:, v * PAD : (v + 1) * PAD]

    def p2_copy(r):
        peer = lax.rem(me + r, PEERS)
        return pltpu.make_async_remote_copy(
            src_ref=p2send.at[:, pl.ds(peer, 1), :],
            dst_ref=p2recv.at[:, pl.ds(me, 1), :],
            send_sem=p2_send.at[r],
            recv_sem=p2_recv,
            device_id={"py": peer},
            device_id_type=MESH,
        )

    def p2_start(r, carry):
        p2_copy(r).start()
        return carry

    lax.fori_loop(1, PEERS, p2_start, 0)
    pltpu.make_async_copy(
        p2send.at[:, pl.ds(me, 1), :], p2recv.at[:, pl.ds(me, 1), :], p2_recv
    ).start()

    for copy in body2:
        copy.wait_recv()
    bsum2[...] = bsum1[...] + bgot2[0] + bgot2[1] + bgot2[2]
    body3 = []
    for r in range(1, 4):
        body3.append(
            pltpu.make_async_remote_copy(
                src_ref=bsum2,
                dst_ref=bgot3.at[r - 1],
                send_sem=b_send.at[3 + r],
                recv_sem=b_recv.at[3 + r],
                device_id={"py": lax.rem(py_in + r, 4) * 8 + px_in * 2 + core},
                device_id_type=MESH,
            )
        )
        body3[-1].start()

    rim_down.wait_recv()
    rim_up.wait_recv()
    rim = trx[:, 32:64, 1152:1280]
    trx[:, 32:64, 1152:1280] = jnp.where(pz == npx - 1, 0.0, rim)
    rim = trx[:, 0:32, 0:128]
    trx[:, 0:32, 0:128] = jnp.where(pz == 0, 0.0, rim)

    mi, mrest = divmod_const(iota((MODES, 256), 0), 25)
    mj = jnp.floor((mrest + 0.5) * 0.2)
    mk = mrest - mj * 5.0
    mode_weight = 8.0 / ((2.0 * mi + 1.0) * (2.0 * mj + 1.0) * (2.0 * mk + 1.0))

    def volume(j, carry):
        base = pl.multiple_of(j * 256, 256)
        cols = pl.ds(base, 256)
        acc = dot(mhh[...], uhl[:, :, cols].reshape(2 * WIDTH, 256)) + dot(
            mlo[...], uhl[0, :, cols]
        )
        scale = mode_weight * jac[:, cols]
        for v in range(NVAR):
            near = jnp.concatenate(
                [trx[v, 0:32, cols], trx[v, 32:64, pl.ds(pl.multiple_of(base + 256, 256), 256)]],
                axis=0,
            )
            high, low = split(near)
            faces = dot(expand_op, jnp.concatenate([high, low], axis=0))
            change = st[v, :, cols] - so[v, :, cols]
            part[v, :, cols] = (
                acc[v * PAD : v * PAD + MODES] + scale * change - penalty[v] * faces[0:MODES]
            )
        return carry

    lax.fori_loop(0, 4, volume, 0)

    load_mass.wait()
    load_oper.wait()

    def split_cut(i, carry):
        rows = pl.ds(pl.multiple_of(i * (8 * CUTS), 8 * CUTS), 8 * CUTS)
        for t in range(2):
            high, low = split(pad_lanes(mats[t, pl.ds(i * 8, 8)].reshape(8 * CUTS, MODES)))
            cuth[rows, t * PAD : (t + 1) * PAD] = high
            cutl[rows, t * PAD : (t + 1) * PAD] = low
        return carry

    lax.fori_loop(0, MODES // 8, split_cut, 0)
    whole = MODES // 8 * 8
    for t in range(2):
        tail = pad_lanes(mats[t, whole:MODES].reshape((MODES - whole) * CUTS, MODES))
        zero = jnp.zeros(((PAD - MODES) * CUTS, PAD), F32)
        high, low = split(jnp.concatenate([tail, zero], axis=0))
        cuth[whole * CUTS :, t * PAD : (t + 1) * PAD] = high
        cutl[whole * CUTS :, t * PAD : (t + 1) * PAD] = low

    pltpu.make_async_copy(p2recv, p2recv, p2_recv).wait()
    xh[...] = jnp.zeros_like(xh)
    xl[...] = jnp.zeros_like(xl)
    take = jnp.where(slot_col == iota((CUTS, SLOTS), 1), 1.0, 0.0)
    take = jnp.concatenate([take, jnp.zeros((CPAD - CUTS, SLOTS), F32)], axis=0).astype(BF16)
    for t in range(2):
        for v in range(NVAR):
            got = jnp.concatenate([p2recv[t * 5 + v], p2recv[10 + t * 5 + v]], axis=0)
            high, low = split(-got if t else got)
            rows, lanes = slice(v * CPAD, (v + 1) * CPAD), slice(t * PAD, (t + 1) * PAD)
            xh[rows, lanes] = dot(take, high).astype(BF16)
            xl[rows, lanes] = dot(take, low).astype(BF16)

    _, block_lane = divmod_const(iota((CUTS, 256), 1), CPAD)
    diagonal = jnp.where(block_lane == iota((CUTS, 256), 0).astype(F32), 1.0, 0.0)

    def products(i, carry):
        rows = pl.ds(pl.multiple_of(i * (MBLOCK * CUTS), MBLOCK * CUTS), MBLOCK * CUTS)
        high, low = cuth[rows, :], cutl[rows, :]
        all_pairs = dot_nt(high, xh[...]) + dot_nt(low, xh[...]) + dot_nt(high, xl[...])
        kept = all_pairs.reshape(MBLOCK, CUTS, 256) * diagonal[None]
        tmode[pl.ds(pl.multiple_of(i * MBLOCK, MBLOCK), MBLOCK), :] = jnp.sum(kept, axis=1)
        return carry

    lax.fori_loop(0, PAD // MBLOCK, products, 0)

    spread_row, spread_lane = divmod_const(iota((CUTS, 256), 1), CPAD)
    spread = jnp.where(spread_lane == iota((CUTS, 256), 0).astype(F32), 1.0, 0.0)
    slots_f = jnp.sum(spread * slot_col.astype(F32), axis=0, keepdims=True)
    lane_v, lane_in = divmod_const(iota((1, 256), 1), CPAD)
    target = jnp.where((lane_in < CUTS) & (lane_v < NVAR), lane_v * SLOTS + slots_f, -1.0)
    place = jnp.where(
        target == iota((NVAR * SLOTS, 256), 0).astype(F32), 1.0, 0.0
    ).astype(BF16)
    high, low = split(tmode[...])
    slotted = dot_nt(place, high) + dot_nt(place, low)
    p3send[...] = slotted.reshape(2 * NVAR, PEERS, PAD)

    def p3_copy(r):
        peer = lax.rem(me + r, PEERS)
        return pltpu.make_async_remote_copy(
            src_ref=p3send.at[:, pl.ds(peer, 1), :],
            dst_ref=p3recv.at[:, pl.ds(me, 1), :],
            send_sem=p3_send.at[r],
            recv_sem=p3_recv,
            device_id={"py": peer},
            device_id_type=MESH,
        )

    def p3_start(r, carry):
        p3_copy(r).start()
        return carry

    lax.fori_loop(1, PEERS, p3_start, 0)
    pltpu.make_async_copy(
        p3send.at[:, pl.ds(me, 1), :], p3recv.at[:, pl.ds(me, 1), :], p3_recv
    ).start()

    for copy in body3:
        copy.wait_recv()
    bodies = bsum2[...] + bgot3[0] + bgot3[1] + bgot3[2]
    tables = []
    for d in range(3):
        x = bodies[d]
        table = [jnp.ones_like(x), x]
        for n in range(1, 4):
            table.append(((2.0 * n + 1.0) * x * table[n] - n * table[n - 1]) / (n + 1.0))
        tables.append(table)
    for i in range(5):
        for j in range(5):
            pair = tables[0][i] * tables[1][j]
            for k in range(5):
                basis[(i * 5 + j) * 5 + k] = pair * tables[2][k]
    for m in range(MODES, PAD):
        basis[m] = jnp.zeros((8, 128), F32)
    for b in range(BODIES):
        rows = slice(b * COVER, (b + 1) * COVER)
        bh, bl = split(basis[:, b, :])
        gh, gl = split(gbody[:, rows, :].reshape(NVAR * COVER, PAD))
        trace = (dot(gh, bh) + dot(gl, bh) + dot(gh, bl)).reshape(NVAR, COVER, 128)
        nx, ny, nz = bodies[3, b : b + 1], bodies[4, b : b + 1], bodies[5, b : b + 1]
        weight = bodies[6, b : b + 1]
        speed = nx * trace[1] + ny * trace[2] + nz * trace[3]
        wall = jnp.concatenate(
            [
                (speed + 0.5 * trace[0]) * weight,
                nx * trace[4] * weight,
                ny * trace[4] * weight,
                nz * trace[4] * weight,
                1.4 * speed * weight,
            ],
            axis=0,
        )
        wh, wl = split(wall)
        lifted = dot_nt(wh, bh) + dot_nt(wl, bh) + dot_nt(wh, bl)
        tbody[:, rows, :] = -lifted.reshape(NVAR, COVER, PAD)

    pltpu.make_async_copy(p3recv, p3recv, p3_recv).wait()
    stores = []
    for v in range(NVAR):
        terms = jnp.concatenate([p3recv[2 * v], p3recv[2 * v + 1], tbody[v]], axis=0)
        high, low = split(terms.T)
        added = dot(high, onehot[...]) + dot(low, onehot[...])
        part[v] = part[v] + added[0:MODES]
        stores.append(pltpu.make_async_copy(part.at[v], out_hbm.at[v], out_sem.at[v]))
        stores[-1].start()

    def finish(r, carry):
        id_copy(r).wait_send()
        p2_copy(r).wait_send()
        p3_copy(r).wait_send()
        return carry

    lax.fori_loop(1, PEERS, finish, 0)
    body1.wait_send()
    for copy in body2 + body3:
        copy.wait_send()
    rim_down.wait_send()
    rim_up.wait_send()
    for copy in stores:
        copy.wait()


def local(
    current_state,
    state_old,
    jacobian,
    volume_operator_list,
    flux_jacobian_list,
    penalty,
    cut_owner,
    cut_element,
    cut_mass,
    cut_operator,
    body_holder_index,
    body_points,
    body_normals,
    body_weights,
    covered,
):
    hbm = pl.BlockSpec(memory_space=pl.ANY)
    vmem = pl.BlockSpec(memory_space=pltpu.VMEM)
    smem = pl.BlockSpec(memory_space=pltpu.SMEM)
    dma = pltpu.SemaphoreType.DMA
    return pl.pallas_call(
        kernel,
        out_shape=jax.ShapeDtypeStruct((NVAR, MODES, ELEM), F32),
        in_specs=[hbm] * 4 + [vmem, vmem, smem, smem, vmem, vmem, smem] + [vmem] * 4,
        out_specs=hbm,
        scratch_shapes=[
            pltpu.VMEM((NVAR, MODES, ELEM), F32),
            pltpu.VMEM((NVAR, MODES, ELEM), F32),
            pltpu.VMEM((2, MODES, CUTS, MODES), F32),
            pltpu.VMEM((2, WIDTH, ELEM), BF16),
            pltpu.VMEM((2, WIDTH, ELEM), BF16),
            pltpu.VMEM((3, PAD, PAD), F32),
            pltpu.VMEM((WIDTH, 2 * WIDTH), BF16),
            pltpu.VMEM((WIDTH, WIDTH), BF16),
            pltpu.VMEM((NVAR, 64, ELEM + 256), F32),
            pltpu.VMEM((NVAR, MODES, ELEM), F32),
            pltpu.VMEM((PAD * CUTS, 256), BF16),
            pltpu.VMEM((PAD * CUTS, 256), BF16),
            pltpu.VMEM((1, 128), jnp.int32),
            pltpu.VMEM((PEERS, 128), jnp.int32),
            pltpu.VMEM((TERMS, ELEM), BF16),
            pltpu.VMEM((4 * NVAR, PEERS, PAD), F32),
            pltpu.VMEM((4 * NVAR, PEERS, PAD), F32),
            pltpu.VMEM((2 * NVAR, PEERS, PAD), F32),
            pltpu.VMEM((2 * NVAR, PEERS, PAD), F32),
            pltpu.VMEM((NVAR, BODIES * COVER, PAD), F32),
            pltpu.VMEM((256, 256), BF16),
            pltpu.VMEM((256, 256), BF16),
            pltpu.VMEM((PAD, 256), F32),
            pltpu.VMEM((7, 8, 128), F32),
            pltpu.VMEM((7, 8, 128), F32),
            pltpu.VMEM((7, 8, 128), F32),
            pltpu.VMEM((3, 7, 8, 128), F32),
            pltpu.VMEM((7, 8, 128), F32),
            pltpu.VMEM((3, 7, 8, 128), F32),
            pltpu.VMEM((PAD, 8, 128), F32),
            pltpu.VMEM((NVAR, BODIES * COVER, PAD), F32),
            dma((4,)),
            dma((NVAR,)),
            dma((2,)),
            dma((2,)),
            dma((PEERS,)),
            dma,
            dma((PEERS,)),
            dma,
            dma((PEERS,)),
            dma,
            dma((7,)),
            dma((7,)),
        ],
        compiler_params=pltpu.CompilerParams(
            collective_id=0, has_side_effects=True, vmem_limit_bytes=56 * 1024 * 1024
        ),
        name="residual_step",
    )(
        current_state,
        state_old,
        cut_mass.transpose(1, 0, 2),
        cut_operator.transpose(1, 0, 2),
        jacobian.reshape(1, ELEM),
        volume_operator_list,
        flux_jacobian_list.transpose(1, 0, 2),
        penalty,
        cut_owner.reshape(1, CUTS),
        cut_element.reshape(1, CUTS),
        body_holder_index,
        body_points,
        body_normals,
        body_weights,
        covered,
    )


def solution(mesh):
    in_specs = (
        P(None, None, ("px", "py")),
        P(None, None, ("px", "py")),
        P(("px", "py")),
        P(),
        P(),
        P(),
        P(("px", "py"), None),
        P(("px", "py")),
        P(("px", "py"), None, None),
        P(("px", "py"), None, None),
        P("px"),
        P(("px", "py"), None, None),
        P(("px", "py"), None, None),
        P(("px", "py"), None),
        P(("px", "py"), None),
    )
    out_specs = P(None, None, ("px", "py"))
    return jax.shard_map(local, mesh=mesh, in_specs=in_specs, out_specs=out_specs, check_vma=False)
```

time: 294 us -> 40.2 us (0.14); the launches traced: 288 us -> 40.1 us
  matrix products: 96 us -> 0 us
  local copies, waits for them, and re-layouts: 93.8 us -> 3.56 us
  waiting for transfers between devices: 44.1 us -> 0 us
  Pallas kernels: 0 us -> 36.5 us
  starting transfers between devices: 22.8 us -> 0 us
  between operations: 18.3 us -> 0.01 us
  other arithmetic: 13.4 us -> 0 us
    dot_general x27 -> x0, matrix products: 96 us -> none  [the longest x3 25.4 us: local(): jnp.einsum('fz,jzx->jfx', volume_operator_list[space_direction], blended_...]
    psum x1 -> x0, waiting for transfers between devices: 44.1 us -> none  [broadcast(): return lax.psum(kept, axis)]
    pallas_call x0 -> x1, Pallas kernels: none -> 36.5 us  [local(): pl.pallas_call(kernel, out_shape=jax.ShapeDtypeStruct((NVAR, MODES, ELEM)...]
    reshape x9 -> x0, local copies, waits for them, and re-layouts: 25.8 us -> none  [the longest x1 6.25 us: local(): jnp.stack([cut_mass, cut_operator], axis=1)]
    dot_general x2 -> x0, local copies, waits for them, and re-layouts: 21.5 us -> none  [local(): lax.dot_general(placing, block_pairs, (((0,), (0,)), ((), ())), precision...]
    all_to_all x2 -> x0, starting transfers between devices: 15.6 us -> none  [the longest x1 8.14 us: local(): lax.all_to_all(packed_ids, 'py', split_axis=0, concat_axis=0, tiled=True)]
    another operation x21 -> x0, local copies, waits for them, and re-layouts: 11.4 us -> none  [the longest x18 7.06 us: legendre_table(): return jnp.stack(poly_table[:DEGREE + 1], axis=0)]
    slice x10 -> x0, local copies, waits for them, and re-layouts: 9.65 us -> none  [the longest x3 2.41 us: local(): normal_x = normals[0][:, None]]
  transfers between devices with their start and end apart: 5 -> 0, of which waited for: 1 -> 0; matrix products, arithmetic and copies ran while one was open for 57% -> 0% of each run, Pallas kernels for 0% -> 0%
where the time goes in v1:
time: 40.2 us; the launch traced here: 40.1 us
  Pallas kernels  36.5 us (91%)
  local copies, waits for them, and re-layouts  3.56 us (9%)
    pallas_call x1, Pallas kernels, local(): pl.pallas_call(kernel, out_shape=jax.ShapeDtypeStruct((NVAR, MODES, ELEM)...  36.5 us
    unnamed x1, local copies, waits for them, and re-layouts  3.56 us

profile of v1, /device:TPU:1, one launch (start us, length us, event | category | flops | bytes accessed | tf_op | source)
XLA Modules:
  0.0 40.1 jit_solution(2293862498679049772)
XLA Ops:
  0.0 36.5 %residual_step.1 = f32[5,125,1024]{2,1,0:T(8,128)} custom-call(f32[5,125,1024]{2,1,0:T(8,128)} %state_hbm.1, f32[5,125,1024]{2,1,0:T(8,128)} %old_hbm.1, f32[125,40,125]{2,1,0:T(8,128)} %bitcast.6, f32[125,40,125]{2,1,0:T(8,128)} %bitcast.7, f32[1,1024]{1,0:T(1,128)} %bitcast.9, f32[3,125,125]{2,1,0:T(8,128)} %vol.1, f32[5,3,5]{2,1,0:T(4,128)} %bitcast.8, ...), custom_call_target="tpu_custom_call" | custom-call | tf_op jit(solution)/shard_map/residual_step/pallas_call | solution.py:567
  36.5 3.6 %copy.17 = f32[5,125,1024]{2,1,0:T(8,128)} copy(f32[5,125,1024]{2,1,0:T(8,128)} %residual_step.1) | data formatting | bytes 5120000

commit v2 on v1

--- a/solution.py
+++ b/solution.py
@@ -74,6 +74,20 @@
     old_hbm,
     mass_hbm,
     oper_hbm,
+    jac_hbm,
+    vol_hbm,
+    flux_hbm,
+    penalty_hbm,
+    owner_hbm,
+    elem_hbm,
+    holder_hbm,
+    points_hbm,
+    normals_hbm,
+    weights_hbm,
+    covered_hbm,
+    part,
+    returned,
+    asked_rows,
     jac,
     vol,
     flux,
@@ -85,7 +99,6 @@
     normals,
     weights,
     covered,
-    out_hbm,
     st,
     so,
     mats,
@@ -95,12 +108,12 @@
     mhh,
     mlo,
     trx,
-    part,
     cuth,
     cutl,
     ids_row,
     ids_all,
     onehot,
+    place,
     p2send,
     p2recv,
     p3send,
@@ -118,7 +131,7 @@
     basis,
     tbody,
     load_sem,
-    out_sem,
+    small_sem,
     rim_send,
     rim_recv,
     id_send,
@@ -134,28 +147,47 @@
     pz = lax.axis_index("px")
     npx = lax.axis_size("px")
 
+    barrier = pltpu.get_barrier_semaphore()
+    above = lax.rem(pz + 1, npx)
+    below = lax.rem(pz + npx - 1, npx)
+
+    def greet(r, carry):
+        pl.semaphore_signal(
+            barrier, inc=1, device_id={"py": lax.rem(me + r, PEERS)}, device_id_type=MESH
+        )
+        return carry
+
+    lax.fori_loop(1, PEERS, greet, 0)
+    for neighbour in (above, below):
+        pl.semaphore_signal(barrier, inc=1, device_id={"px": neighbour}, device_id_type=MESH)
+
     load_state = pltpu.make_async_copy(state_hbm, st, load_sem.at[0])
     load_old = pltpu.make_async_copy(old_hbm, so, load_sem.at[1])
     load_mass = pltpu.make_async_copy(mass_hbm, mats.at[0], load_sem.at[2])
     load_oper = pltpu.make_async_copy(oper_hbm, mats.at[1], load_sem.at[3])
+    pairs = (
+        (owner_hbm, owner),
+        (elem_hbm, elem),
+        (covered_hbm, covered),
+        (holder_hbm, holder),
+        (points_hbm, points),
+        (normals_hbm, normals),
+        (weights_hbm, weights),
+        (penalty_hbm, penalty),
+        (flux_hbm, flux),
+        (vol_hbm, vol),
+        (jac_hbm, jac),
+    )
+    smalls = [
+        pltpu.make_async_copy(source, target, small_sem.at[i])
+        for i, (source, target) in enumerate(pairs)
+    ]
+    for copy in smalls:
+        copy.start()
+    for copy in smalls:
+        copy.wait()
     load_state.start()
     load_old.start()
-    load_mass.start()
-    load_oper.start()
-
-    barrier = pltpu.get_barrier_semaphore()
-    above = lax.rem(pz + 1, npx)
-    below = lax.rem(pz + npx - 1, npx)
-
-    def greet(r, carry):
-        pl.semaphore_signal(
-            barrier, inc=1, device_id={"py": lax.rem(me + r, PEERS)}, device_id_type=MESH
-        )
-        return carry
-
-    lax.fori_loop(1, PEERS, greet, 0)
-    for neighbour in (above, below):
-        pl.semaphore_signal(barrier, inc=1, device_id={"px": neighbour}, device_id_type=MESH)
 
     own_row = jnp.broadcast_to(owner[...], (CUTS, CUTS))
     own_col = to_column(owner[...], CUTS, CUTS)
@@ -169,6 +201,21 @@
     placed = jnp.where(slot_col == iota((CUTS, PAD), 1), elem_col + 1, 0)
     ids_row[...] = jnp.sum(placed, axis=0, keepdims=True) - 1
 
+    _, spread_lane = divmod_const(iota((CUTS, 256), 1), CPAD)
+    spread = jnp.where(spread_lane == iota((CUTS, 256), 0).astype(F32), 1.0, 0.0)
+    slots_f = jnp.sum(spread * slot_col.astype(F32), axis=0, keepdims=True)
+    lane_v, lane_in = divmod_const(iota((1, 256), 1), CPAD)
+    target = jnp.where((lane_in < CUTS) & (lane_v < NVAR), lane_v * SLOTS + slots_f, -1.0)
+    place[...] = jnp.where(
+        target == iota((NVAR * SLOTS, 256), 0).astype(F32), 1.0, 0.0
+    ).astype(BF16)
+
+    cover_lane = iota((COVER, ELEM), 1)
+    for b in range(BODIES):
+        wanted = to_column(covered[b : b + 1, :], COVER, COVER)
+        start = SLOTS + b * COVER
+        onehot[start : start + COVER, :] = jnp.where(wanted == cover_lane, 1.0, 0.0).astype(BF16)
+
     bown[...] = jnp.zeros_like(bown)
     body_row = iota((BODIES, 128), 0)
     held = jnp.zeros((BODIES, 128), jnp.int32)
@@ -179,6 +226,41 @@
         bown[d, 0:BODIES, :] = jnp.where(held, points[:, d, :], 0.0)
         bown[3 + d, 0:BODIES, :] = jnp.where(held, normals[:, d, :], 0.0)
     bown[6, 0:BODIES, :] = jnp.where(held, weights[...], 0.0)
+
+    ri, rf = divmod_const(iota((PAD, PAD), 0), 25)
+    ti, tf = divmod_const(iota((64, PAD), 1), 25)
+    tr_row = iota((64, PAD), 0)
+    tr_lower = tr_row >= 32
+    tr_f = jnp.where(tr_lower, tr_row - 32, tr_row).astype(F32)
+    trace_op = jnp.where(
+        (tf == tr_f) & (ti < 5.0), jnp.where(tr_lower, parity_of(ti), 1.0), 0.0
+    ).astype(BF16)
+    l64 = lax.rem(iota((PAD, PAD), 1), 64)
+    l32 = lax.rem(iota((PAD, PAD), 1), 32)
+    expand_op = jnp.where(
+        (rf == l32.astype(F32)) & (ri < 5.0), jnp.where(l64 < 32, parity_of(ri), 1.0), 0.0
+    ).astype(BF16)
+
+    vpad[...] = jnp.zeros_like(vpad)
+    for d in range(3):
+        vpad[d, 0:MODES, 0:MODES] = vol[d]
+    ci, cf = divmod_const(iota((PAD, PAD), 1), 25)
+    inside = (ri < 5.0) & (ci < 5.0)
+    own_face = jnp.where(inside & (rf == cf), 1.0 + parity_of(ri) * parity_of(ci), 0.0)
+
+    def build(v, carry):
+        rows = pl.ds(pl.multiple_of(v * PAD, PAD), PAD)
+        for w in range(NVAR):
+            block = jnp.where(v == w, penalty[v], 0.0) * own_face
+            for d in range(3):
+                block = block - flux[v, d, w] * vpad[d]
+            high, low = split(block)
+            mhh[rows, w * PAD : (w + 1) * PAD] = high
+            mhh[rows, WIDTH + w * PAD : WIDTH + (w + 1) * PAD] = high
+            mlo[rows, w * PAD : (w + 1) * PAD] = low
+        return carry
+
+    lax.fori_loop(0, NVAR, build, 0)
 
     pl.semaphore_wait(barrier, PEERS + 1)
 
@@ -213,43 +295,10 @@
     )
     body1.start()
 
-    vpad[...] = jnp.zeros_like(vpad)
-    for d in range(3):
-        vpad[d, 0:MODES, 0:MODES] = vol[d]
-    ri, rf = divmod_const(iota((PAD, PAD), 0), 25)
-    ci, cf = divmod_const(iota((PAD, PAD), 1), 25)
-    inside = (ri < 5.0) & (ci < 5.0)
-    own_face = jnp.where(inside & (rf == cf), 1.0 + parity_of(ri) * parity_of(ci), 0.0)
-
-    def build(v, carry):
-        rows = pl.ds(pl.multiple_of(v * PAD, PAD), PAD)
-        for w in range(NVAR):
-            block = jnp.where(v == w, penalty[v], 0.0) * own_face
-            for d in range(3):
-                block = block - flux[v, d, w] * vpad[d]
-            high, low = split(block)
-            mhh[rows, w * PAD : (w + 1) * PAD] = high
-            mhh[rows, WIDTH + w * PAD : WIDTH + (w + 1) * PAD] = high
-            mlo[rows, w * PAD : (w + 1) * PAD] = low
-        return carry
-
-    lax.fori_loop(0, NVAR, build, 0)
-
-    ti, tf = divmod_const(iota((64, PAD), 1), 25)
-    tr_row = iota((64, PAD), 0)
-    tr_lower = tr_row >= 32
-    tr_f = jnp.where(tr_lower, tr_row - 32, tr_row).astype(F32)
-    trace_op = jnp.where(
-        (tf == tr_f) & (ti < 5.0), jnp.where(tr_lower, parity_of(ti), 1.0), 0.0
-    ).astype(BF16)
-    l64 = lax.rem(iota((PAD, PAD), 1), 64)
-    l32 = lax.rem(iota((PAD, PAD), 1), 32)
-    expand_op = jnp.where(
-        (rf == l32.astype(F32)) & (ri < 5.0), jnp.where(l64 < 32, parity_of(ri), 1.0), 0.0
-    ).astype(BF16)
-
     load_state.wait()
     load_old.wait()
+    load_mass.start()
+    load_oper.start()
 
     def split_state(j, carry):
         cols = pl.ds(pl.multiple_of(j * 256, 256), 256)
@@ -267,7 +316,6 @@
         return carry
 
     lax.fori_loop(0, 4, split_state, 0)
-
     rim_down = pltpu.make_async_remote_copy(
         src_ref=trx.at[:, 32:64, 128:256],
         dst_ref=trx.at[:, 32:64, 1152:1280],
@@ -303,19 +351,34 @@
         )
         body2[-1].start()
 
+    load_mass.wait()
+    load_oper.wait()
+
+    def split_cut(i, carry):
+        rows = pl.ds(pl.multiple_of(i * (8 * CUTS), 8 * CUTS), 8 * CUTS)
+        for t in range(2):
+            high, low = split(pad_lanes(mats[t, pl.ds(i * 8, 8)].reshape(8 * CUTS, MODES)))
+            cuth[rows, t * PAD : (t + 1) * PAD] = high
+            cutl[rows, t * PAD : (t + 1) * PAD] = low
+        return carry
+
+    lax.fori_loop(0, MODES // 8, split_cut, 0)
+    whole = MODES // 8 * 8
+    for t in range(2):
+        tail = pad_lanes(mats[t, whole:MODES].reshape((MODES - whole) * CUTS, MODES))
+        zero = jnp.zeros(((PAD - MODES) * CUTS, PAD), F32)
+        high, low = split(jnp.concatenate([tail, zero], axis=0))
+        cuth[whole * CUTS :, t * PAD : (t + 1) * PAD] = high
+        cutl[whole * CUTS :, t * PAD : (t + 1) * PAD] = low
+
     pltpu.make_async_copy(ids_all, ids_all, id_recv).wait()
     asked = ids_all[...]
     lane = iota((PEERS, 128), 1)
     elem_lane = iota((PEERS, ELEM), 1)
     for k in range(2):
         wanted = jnp.sum(jnp.where(lane == me + k * PEERS, asked, 0), axis=1, keepdims=True)
-        onehot[k * PEERS : (k + 1) * PEERS, :] = jnp.where(wanted == elem_lane, 1.0, 0.0).astype(BF16)
-    cover_lane = iota((COVER, ELEM), 1)
-    for b in range(BODIES):
-        wanted = to_column(covered[b : b + 1, :], COVER, COVER)
-        start = SLOTS + b * COVER
-        onehot[start : start + COVER, :] = jnp.where(wanted == cover_lane, 1.0, 0.0).astype(BF16)
-
+        rows = slice(k * PEERS, (k + 1) * PEERS)
+        onehot[rows, :] = jnp.where(wanted == elem_lane, 1.0, 0.0).astype(BF16)
     state_high = dot_nt(onehot[...], uhl[0])
     state_low = dot_nt(onehot[...], uhl[1])
     state_cols = state_high + state_low
@@ -399,84 +462,6 @@
         return carry
 
     lax.fori_loop(0, 4, volume, 0)
-
-    load_mass.wait()
-    load_oper.wait()
-
-    def split_cut(i, carry):
-        rows = pl.ds(pl.multiple_of(i * (8 * CUTS), 8 * CUTS), 8 * CUTS)
-        for t in range(2):
-            high, low = split(pad_lanes(mats[t, pl.ds(i * 8, 8)].reshape(8 * CUTS, MODES)))
-            cuth[rows, t * PAD : (t + 1) * PAD] = high
-            cutl[rows, t * PAD : (t + 1) * PAD] = low
-        return carry
-
-    lax.fori_loop(0, MODES // 8, split_cut, 0)
-    whole = MODES // 8 * 8
-    for t in range(2):
-        tail = pad_lanes(mats[t, whole:MODES].reshape((MODES - whole) * CUTS, MODES))
-        zero = jnp.zeros(((PAD - MODES) * CUTS, PAD), F32)
-        high, low = split(jnp.concatenate([tail, zero], axis=0))
-        cuth[whole * CUTS :, t * PAD : (t + 1) * PAD] = high
-        cutl[whole * CUTS :, t * PAD : (t + 1) * PAD] = low
-
-    pltpu.make_async_copy(p2recv, p2recv, p2_recv).wait()
-    xh[...] = jnp.zeros_like(xh)
-    xl[...] = jnp.zeros_like(xl)
-    take = jnp.where(slot_col == iota((CUTS, SLOTS), 1), 1.0, 0.0)
-    take = jnp.concatenate([take, jnp.zeros((CPAD - CUTS, SLOTS), F32)], axis=0).astype(BF16)
-    for t in range(2):
-        for v in range(NVAR):
-            got = jnp.concatenate([p2recv[t * 5 + v], p2recv[10 + t * 5 + v]], axis=0)
-            high, low = split(-got if t else got)
-            rows, lanes = slice(v * CPAD, (v + 1) * CPAD), slice(t * PAD, (t + 1) * PAD)
-            xh[rows, lanes] = dot(take, high).astype(BF16)
-            xl[rows, lanes] = dot(take, low).astype(BF16)
-
-    _, block_lane = divmod_const(iota((CUTS, 256), 1), CPAD)
-    diagonal = jnp.where(block_lane == iota((CUTS, 256), 0).astype(F32), 1.0, 0.0)
-
-    def products(i, carry):
-        rows = pl.ds(pl.multiple_of(i * (MBLOCK * CUTS), MBLOCK * CUTS), MBLOCK * CUTS)
-        high, low = cuth[rows, :], cutl[rows, :]
-        all_pairs = dot_nt(high, xh[...]) + dot_nt(low, xh[...]) + dot_nt(high, xl[...])
-        kept = all_pairs.reshape(MBLOCK, CUTS, 256) * diagonal[None]
-        tmode[pl.ds(pl.multiple_of(i * MBLOCK, MBLOCK), MBLOCK), :] = jnp.sum(kept, axis=1)
-        return carry
-
-    lax.fori_loop(0, PAD // MBLOCK, products, 0)
-
-    spread_row, spread_lane = divmod_const(iota((CUTS, 256), 1), CPAD)
-    spread = jnp.where(spread_lane == iota((CUTS, 256), 0).astype(F32), 1.0, 0.0)
-    slots_f = jnp.sum(spread * slot_col.astype(F32), axis=0, keepdims=True)
-    lane_v, lane_in = divmod_const(iota((1, 256), 1), CPAD)
-    target = jnp.where((lane_in < CUTS) & (lane_v < NVAR), lane_v * SLOTS + slots_f, -1.0)
-    place = jnp.where(
-        target == iota((NVAR * SLOTS, 256), 0).astype(F32), 1.0, 0.0
-    ).astype(BF16)
-    high, low = split(tmode[...])
-    slotted = dot_nt(place, high) + dot_nt(place, low)
-    p3send[...] = slotted.reshape(2 * NVAR, PEERS, PAD)
-
-    def p3_copy(r):
-        peer = lax.rem(me + r, PEERS)
-        return pltpu.make_async_remote_copy(
-            src_ref=p3send.at[:, pl.ds(peer, 1), :],
-            dst_ref=p3recv.at[:, pl.ds(me, 1), :],
-            send_sem=p3_send.at[r],
-            recv_sem=p3_recv,
-            device_id={"py": peer},
-            device_id_type=MESH,
-        )
-
-    def p3_start(r, carry):
-        p3_copy(r).start()
-        return carry
-
-    lax.fori_loop(1, PEERS, p3_start, 0)
-    pltpu.make_async_copy(
-        p3send.at[:, pl.ds(me, 1), :], p3recv.at[:, pl.ds(me, 1), :], p3_recv
-    ).start()
 
     for copy in body3:
         copy.wait_recv()
@@ -517,15 +502,65 @@
         lifted = dot_nt(wh, bh) + dot_nt(wl, bh) + dot_nt(wh, bl)
         tbody[:, rows, :] = -lifted.reshape(NVAR, COVER, PAD)
 
+    pltpu.make_async_copy(p2recv, p2recv, p2_recv).wait()
+    xh[...] = jnp.zeros_like(xh)
+    xl[...] = jnp.zeros_like(xl)
+    take = jnp.where(slot_col == iota((CUTS, SLOTS), 1), 1.0, 0.0)
+    take = jnp.concatenate([take, jnp.zeros((CPAD - CUTS, SLOTS), F32)], axis=0).astype(BF16)
+    for t in range(2):
+        for v in range(NVAR):
+            got = jnp.concatenate([p2recv[t * 5 + v], p2recv[10 + t * 5 + v]], axis=0)
+            high, low = split(-got if t else got)
+            rows, lanes = slice(v * CPAD, (v + 1) * CPAD), slice(t * PAD, (t + 1) * PAD)
+            xh[rows, lanes] = dot(take, high).astype(BF16)
+            xl[rows, lanes] = dot(take, low).astype(BF16)
+
+    _, block_lane = divmod_const(iota((CUTS, 256), 1), CPAD)
+    diagonal = jnp.where(block_lane == iota((CUTS, 256), 0).astype(F32), 1.0, 0.0)
+
+    def products(i, carry):
+        rows = pl.ds(pl.multiple_of(i * (MBLOCK * CUTS), MBLOCK * CUTS), MBLOCK * CUTS)
+        high, low = cuth[rows, :], cutl[rows, :]
+        all_pairs = dot_nt(high, xh[...]) + dot_nt(low, xh[...]) + dot_nt(high, xl[...])
+        kept = all_pairs.reshape(MBLOCK, CUTS, 256) * diagonal[None]
+        tmode[pl.ds(pl.multiple_of(i * MBLOCK, MBLOCK), MBLOCK), :] = jnp.sum(kept, axis=1)
+        return carry
+
+    lax.fori_loop(0, PAD // MBLOCK, products, 0)
+
+    high, low = split(tmode[...])
+    slotted = dot_nt(place[...], high) + dot_nt(place[...], low)
+    p3send[...] = slotted.reshape(2 * NVAR, PEERS, PAD)
+
+    def p3_copy(r):
+        peer = lax.rem(me + r, PEERS)
+        return pltpu.make_async_remote_copy(
+            src_ref=p3send.at[:, pl.ds(peer, 1), :],
+            dst_ref=p3recv.at[:, pl.ds(me, 1), :],
+            send_sem=p3_send.at[r],
+            recv_sem=p3_recv,
+            device_id={"py": peer},
+            device_id_type=MESH,
+        )
+
+    def p3_start(r, carry):
+        p3_copy(r).start()
+        return carry
+
+    lax.fori_loop(1, PEERS, p3_start, 0)
+    pltpu.make_async_copy(
+        p3send.at[:, pl.ds(me, 1), :], p3recv.at[:, pl.ds(me, 1), :], p3_recv
+    ).start()
+
+    for v in range(NVAR):
+        high, low = split(tbody[v].T)
+        cover = onehot[SLOTS:, :]
+        added = dot(high, cover) + dot(low, cover)
+        part[v] = part[v] + added[0:MODES]
+
+    asked_rows[...] = onehot[0:SLOTS, :]
     pltpu.make_async_copy(p3recv, p3recv, p3_recv).wait()
-    stores = []
-    for v in range(NVAR):
-        terms = jnp.concatenate([p3recv[2 * v], p3recv[2 * v + 1], tbody[v]], axis=0)
-        high, low = split(terms.T)
-        added = dot(high, onehot[...]) + dot(low, onehot[...])
-        part[v] = part[v] + added[0:MODES]
-        stores.append(pltpu.make_async_copy(part.at[v], out_hbm.at[v], out_sem.at[v]))
-        stores[-1].start()
+    returned[...] = p3recv[...]
 
     def finish(r, carry):
         id_copy(r).wait_send()
@@ -539,6 +574,17 @@
         copy.wait_send()
     rim_down.wait_send()
     rim_up.wait_send()
+
+
+def add_cut_terms(part, got, asked_rows, out_hbm, total, out_sem):
+    stores = []
+    for v in range(NVAR):
+        terms = jnp.concatenate([got[2 * v], got[2 * v + 1]], axis=0)
+        high, low = split(terms.T)
+        added = dot(high, asked_rows[...]) + dot(low, asked_rows[...])
+        total[v] = part[v] + added[0:MODES]
+        stores.append(pltpu.make_async_copy(total.at[v], out_hbm.at[v], out_sem.at[v]))
+        stores[-1].start()
     for copy in stores:
         copy.wait()
 
@@ -561,15 +607,46 @@
     covered,
 ):
     hbm = pl.BlockSpec(memory_space=pl.ANY)
+    dma = pltpu.SemaphoreType.DMA
     vmem = pl.BlockSpec(memory_space=pltpu.VMEM)
-    smem = pl.BlockSpec(memory_space=pltpu.SMEM)
-    dma = pltpu.SemaphoreType.DMA
-    return pl.pallas_call(
+    operands = (
+        current_state,
+        state_old,
+        cut_mass.transpose(1, 0, 2),
+        cut_operator.transpose(1, 0, 2),
+        jacobian.reshape(1, ELEM),
+        volume_operator_list,
+        flux_jacobian_list.transpose(1, 0, 2),
+        penalty,
+        cut_owner.reshape(1, CUTS),
+        cut_element.reshape(1, CUTS),
+        body_holder_index,
+        body_points,
+        body_normals,
+        body_weights,
+        covered,
+    )
+    partial = pl.pallas_call(
         kernel,
-        out_shape=jax.ShapeDtypeStruct((NVAR, MODES, ELEM), F32),
-        in_specs=[hbm] * 4 + [vmem, vmem, smem, smem, vmem, vmem, smem] + [vmem] * 4,
-        out_specs=hbm,
+        out_shape=(
+            pltpu.VMEM((NVAR, MODES, ELEM), F32),
+            pltpu.VMEM((2 * NVAR, PEERS, PAD), F32),
+            pltpu.VMEM((SLOTS, ELEM), BF16),
+        ),
+        in_specs=[hbm] * 15,
+        out_specs=(vmem, vmem, vmem),
         scratch_shapes=[
+            pltpu.VMEM((1, ELEM), F32),
+            pltpu.VMEM((3, MODES, MODES), F32),
+            pltpu.SMEM((NVAR, 3, NVAR), F32),
+            pltpu.SMEM((NVAR,), F32),
+            pltpu.VMEM((1, CUTS), jnp.int32),
+            pltpu.VMEM((1, CUTS), jnp.int32),
+            pltpu.SMEM((BODIES,), jnp.int32),
+            pltpu.VMEM((BODIES, 3, 128), F32),
+            pltpu.VMEM((BODIES, 3, 128), F32),
+            pltpu.VMEM((BODIES, 128), F32),
+            pltpu.VMEM((BODIES, COVER), jnp.int32),
             pltpu.VMEM((NVAR, MODES, ELEM), F32),
             pltpu.VMEM((NVAR, MODES, ELEM), F32),
             pltpu.VMEM((2, MODES, CUTS, MODES), F32),
@@ -579,12 +656,12 @@
             pltpu.VMEM((WIDTH, 2 * WIDTH), BF16),
             pltpu.VMEM((WIDTH, WIDTH), BF16),
             pltpu.VMEM((NVAR, 64, ELEM + 256), F32),
-            pltpu.VMEM((NVAR, MODES, ELEM), F32),
             pltpu.VMEM((PAD * CUTS, 256), BF16),
             pltpu.VMEM((PAD * CUTS, 256), BF16),
             pltpu.VMEM((1, 128), jnp.int32),
             pltpu.VMEM((PEERS, 128), jnp.int32),
             pltpu.VMEM((TERMS, ELEM), BF16),
+            pltpu.VMEM((NVAR * SLOTS, 256), BF16),
             pltpu.VMEM((4 * NVAR, PEERS, PAD), F32),
             pltpu.VMEM((4 * NVAR, PEERS, PAD), F32),
             pltpu.VMEM((2 * NVAR, PEERS, PAD), F32),
@@ -602,7 +679,7 @@
             pltpu.VMEM((PAD, 8, 128), F32),
             pltpu.VMEM((NVAR, BODIES * COVER, PAD), F32),
             dma((4,)),
-            dma((NVAR,)),
+            dma((11,)),
             dma((2,)),
             dma((2,)),
             dma((PEERS,)),
@@ -615,26 +692,21 @@
             dma((7,)),
         ],
         compiler_params=pltpu.CompilerParams(
-            collective_id=0, has_side_effects=True, vmem_limit_bytes=56 * 1024 * 1024
+            collective_id=0, has_side_effects=True, vmem_limit_bytes=44 * 1024 * 1024
         ),
         name="residual_step",
     )(
-        current_state,
-        state_old,
-        cut_mass.transpose(1, 0, 2),
-        cut_operator.transpose(1, 0, 2),
-        jacobian.reshape(1, ELEM),
-        volume_operator_list,
-        flux_jacobian_list.transpose(1, 0, 2),
-        penalty,
-        cut_owner.reshape(1, CUTS),
-        cut_element.reshape(1, CUTS),
-        body_holder_index,
-        body_points,
-        body_normals,
-        body_weights,
-        covered,
+        *(pltpu.with_memory_space_constraint(x, pltpu.HBM) for x in operands)
     )
+    return pl.pallas_call(
+        add_cut_terms,
+        out_shape=jax.ShapeDtypeStruct((NVAR, MODES, ELEM), F32),
+        in_specs=[vmem] * 3,
+        out_specs=hbm,
+        scratch_shapes=[pltpu.VMEM((NVAR, MODES, ELEM), F32), dma((NVAR,))],
+        compiler_params=pltpu.CompilerParams(vmem_limit_bytes=16 * 1024 * 1024),
+        name="add_cut_terms",
+    )(*partial)
 
 
 def solution(mesh):

time: 40.2 us -> 37 us (0.920)
  local copies, waits for them, and re-layouts: 3.56 us -> 0 us
    unnamed x1 -> x0, local copies, waits for them, and re-layouts: 3.56 us -> none
    pallas_call x1 -> x2, Pallas kernels: 36.5 us -> 36.9 us  [the longest x1 35 us: local(): pl.pallas_call(kernel, out_shape=(pltpu.VMEM((NVAR, MODES, ELEM), F32), p...]
where the time goes in v2:
time: 37 us; the launch traced here: 36.9 us
  Pallas kernels  36.9 us (100%)
    pallas_call x1, Pallas kernels, local(): pl.pallas_call(kernel, out_shape=(pltpu.VMEM((NVAR, MODES, ELEM), F32), p...  35 us
    pallas_call x1, Pallas kernels, local(): pl.pallas_call(add_cut_terms, out_shape=jax.ShapeDtypeStruct((NVAR, MODES...  1.87 us

profile of v2, /device:TPU:1, one launch (start us, length us, event | category | flops | bytes accessed | tf_op | source)
XLA Modules:
  0.0 36.9 jit_solution(2958636865597810543)
XLA Ops:
  0.0 35.0 %residual_step.1 = (f32[5,125,1024]{2,1,0:T(8,128)S(1)}, f32[10,32,128]{2,1,0:T(8,128)S(1)}, bf16[64,1024]{1,0:T(8,128)(2,1)S(1)}) custom-call(f32[5,125,1024]{2,1,0:T(8,128)} %state_hbm.1, f32[5,125,1024]{2,1,0:T(8,128)} %old_hbm.1, f32[125,40,125]{2,1,0:T(8,128)} %bitcast.6, f32[125,40,125]{2,1,0:T(8,128)} %bitcast.7, f32[1,1024]{1,0:T(1,128)} %bitcast.9, ...), custom_call_target="tpu_custom_call" | custom-call | tf_op jit(solution)/shard_map/residual_step/pallas_call | solution.py:629
  35.0 1.9 %add_cut_terms.1 = f32[5,125,1024]{2,1,0:T(8,128)} custom-call(f32[5,125,1024]{2,1,0:T(8,128)S(1)} %get-tuple-element.8.part, f32[10,32,128]{2,1,0:T(8,128)S(1)} %get-tuple-element.9.got, bf16[64,1024]{1,0:T(8,128)(2,1)S(1)} %get-tuple-element.10.asked_rows), custom_call_target="tpu_custom_call" | custom-call | tf_op jit(solution)/shard_map/add_cut_terms/pallas_call | solution.py:701

commit v3 on v2

--- a/solution.py
+++ b/solution.py
@@ -22,7 +22,7 @@
 COVER = 16
 TERMS = SLOTS + BODIES * COVER
 WIDTH = NVAR * PAD
-MBLOCK = 16
+MBLOCK = 64
 
 
 def split(value):
@@ -463,6 +463,53 @@
 
     lax.fori_loop(0, 4, volume, 0)
 
+    pltpu.make_async_copy(p2recv, p2recv, p2_recv).wait()
+    xh[...] = jnp.zeros_like(xh)
+    xl[...] = jnp.zeros_like(xl)
+    take = jnp.where(slot_col == iota((CUTS, SLOTS), 1), 1.0, 0.0)
+    take = jnp.concatenate([take, jnp.zeros((CPAD - CUTS, SLOTS), F32)], axis=0).astype(BF16)
+    for t in range(2):
+        for v in range(NVAR):
+            got = jnp.concatenate([p2recv[t * 5 + v], p2recv[10 + t * 5 + v]], axis=0)
+            high, low = split(-got if t else got)
+            rows, lanes = slice(v * CPAD, (v + 1) * CPAD), slice(t * PAD, (t + 1) * PAD)
+            xh[rows, lanes] = dot(take, high).astype(BF16)
+            xl[rows, lanes] = dot(take, low).astype(BF16)
+
+    _, block_lane = divmod_const(iota((CUTS, 256), 1), CPAD)
+    diagonal = jnp.where(block_lane == iota((CUTS, 256), 0).astype(F32), 1.0, 0.0)
+
+    for i in range(PAD // MBLOCK):
+        rows = slice(i * MBLOCK * CUTS, (i + 1) * MBLOCK * CUTS)
+        high, low = cuth[rows, :], cutl[rows, :]
+        all_pairs = dot_nt(high, xh[...]) + (dot_nt(low, xh[...]) + dot_nt(high, xl[...]))
+        kept = all_pairs.reshape(MBLOCK, CUTS, 256) * diagonal[None]
+        tmode[i * MBLOCK : (i + 1) * MBLOCK, :] = jnp.sum(kept, axis=1)
+
+    high, low = split(tmode[...])
+    slotted = dot_nt(place[...], high) + dot_nt(place[...], low)
+    p3send[...] = slotted.reshape(2 * NVAR, PEERS, PAD)
+
+    def p3_copy(r):
+        peer = lax.rem(me + r, PEERS)
+        return pltpu.make_async_remote_copy(
+            src_ref=p3send.at[:, pl.ds(peer, 1), :],
+            dst_ref=p3recv.at[:, pl.ds(me, 1), :],
+            send_sem=p3_send.at[r],
+            recv_sem=p3_recv,
+            device_id={"py": peer},
+            device_id_type=MESH,
+        )
+
+    def p3_start(r, carry):
+        p3_copy(r).start()
+        return carry
+
+    lax.fori_loop(1, PEERS, p3_start, 0)
+    pltpu.make_async_copy(
+        p3send.at[:, pl.ds(me, 1), :], p3recv.at[:, pl.ds(me, 1), :], p3_recv
+    ).start()
+
     for copy in body3:
         copy.wait_recv()
     bodies = bsum2[...] + bgot3[0] + bgot3[1] + bgot3[2]
@@ -502,86 +549,41 @@
         lifted = dot_nt(wh, bh) + dot_nt(wl, bh) + dot_nt(wh, bl)
         tbody[:, rows, :] = -lifted.reshape(NVAR, COVER, PAD)
 
-    pltpu.make_async_copy(p2recv, p2recv, p2_recv).wait()
-    xh[...] = jnp.zeros_like(xh)
-    xl[...] = jnp.zeros_like(xl)
-    take = jnp.where(slot_col == iota((CUTS, SLOTS), 1), 1.0, 0.0)
-    take = jnp.concatenate([take, jnp.zeros((CPAD - CUTS, SLOTS), F32)], axis=0).astype(BF16)
-    for t in range(2):
-        for v in range(NVAR):
-            got = jnp.concatenate([p2recv[t * 5 + v], p2recv[10 + t * 5 + v]], axis=0)
-            high, low = split(-got if t else got)
-            rows, lanes = slice(v * CPAD, (v + 1) * CPAD), slice(t * PAD, (t + 1) * PAD)
-            xh[rows, lanes] = dot(take, high).astype(BF16)
-            xl[rows, lanes] = dot(take, low).astype(BF16)
-
-    _, block_lane = divmod_const(iota((CUTS, 256), 1), CPAD)
-    diagonal = jnp.where(block_lane == iota((CUTS, 256), 0).astype(F32), 1.0, 0.0)
-
-    def products(i, carry):
-        rows = pl.ds(pl.multiple_of(i * (MBLOCK * CUTS), MBLOCK * CUTS), MBLOCK * CUTS)
-        high, low = cuth[rows, :], cutl[rows, :]
-        all_pairs = dot_nt(high, xh[...]) + dot_nt(low, xh[...]) + dot_nt(high, xl[...])
-        kept = all_pairs.reshape(MBLOCK, CUTS, 256) * diagonal[None]
-        tmode[pl.ds(pl.multiple_of(i * MBLOCK, MBLOCK), MBLOCK), :] = jnp.sum(kept, axis=1)
-        return carry
-
-    lax.fori_loop(0, PAD // MBLOCK, products, 0)
-
-    high, low = split(tmode[...])
-    slotted = dot_nt(place[...], high) + dot_nt(place[...], low)
-    p3send[...] = slotted.reshape(2 * NVAR, PEERS, PAD)
-
-    def p3_copy(r):
-        peer = lax.rem(me + r, PEERS)
-        return pltpu.make_async_remote_copy(
-            src_ref=p3send.at[:, pl.ds(peer, 1), :],
-            dst_ref=p3recv.at[:, pl.ds(me, 1), :],
-            send_sem=p3_send.at[r],
-            recv_sem=p3_recv,
-            device_id={"py": peer},
-            device_id_type=MESH,
-        )
-
-    def p3_start(r, carry):
-        p3_copy(r).start()
-        return carry
-
-    lax.fori_loop(1, PEERS, p3_start, 0)
-    pltpu.make_async_copy(
-        p3send.at[:, pl.ds(me, 1), :], p3recv.at[:, pl.ds(me, 1), :], p3_recv
-    ).start()
-
     for v in range(NVAR):
         high, low = split(tbody[v].T)
         cover = onehot[SLOTS:, :]
         added = dot(high, cover) + dot(low, cover)
         part[v] = part[v] + added[0:MODES]
 
-    asked_rows[...] = onehot[0:SLOTS, :]
-    pltpu.make_async_copy(p3recv, p3recv, p3_recv).wait()
-    returned[...] = p3recv[...]
-
-    def finish(r, carry):
+    def left_before(r, carry):
         id_copy(r).wait_send()
         p2_copy(r).wait_send()
-        p3_copy(r).wait_send()
-        return carry
-
-    lax.fori_loop(1, PEERS, finish, 0)
+        return carry
+
+    lax.fori_loop(1, PEERS, left_before, 0)
     body1.wait_send()
     for copy in body2 + body3:
         copy.wait_send()
     rim_down.wait_send()
     rim_up.wait_send()
+    asked_rows[...] = onehot[0:SLOTS, :]
+
+    pltpu.make_async_copy(p3recv, p3recv, p3_recv).wait()
+    returned[...] = p3recv[...]
+
+    def left(r, carry):
+        p3_copy(r).wait_send()
+        return carry
+
+    lax.fori_loop(1, PEERS, left, 0)
 
 
 def add_cut_terms(part, got, asked_rows, out_hbm, total, out_sem):
+    rows = jnp.concatenate([asked_rows[...], asked_rows[...]], axis=0)
     stores = []
     for v in range(NVAR):
         terms = jnp.concatenate([got[2 * v], got[2 * v + 1]], axis=0)
-        high, low = split(terms.T)
-        added = dot(high, asked_rows[...]) + dot(low, asked_rows[...])
+        added = dot(jnp.concatenate(split(terms.T), axis=1), rows)
         total[v] = part[v] + added[0:MODES]
         stores.append(pltpu.make_async_copy(total.at[v], out_hbm.at[v], out_sem.at[v]))
         stores[-1].start()

time: 37 us -> 34.2 us (0.924)
  Pallas kernels: 36.9 us -> 34.1 us
    pallas_call x1, Pallas kernels: 35 us -> 32.2 us  [local(): pl.pallas_call(kernel, out_shape=(pltpu.VMEM((NVAR, MODES, ELEM), F32), p...]
where the time goes in v3:
time: 34.2 us; the launch traced here: 34.1 us
  Pallas kernels  34.1 us (100%)
    pallas_call x1, Pallas kernels, local(): pl.pallas_call(kernel, out_shape=(pltpu.VMEM((NVAR, MODES, ELEM), F32), p...  32.2 us
    pallas_call x1, Pallas kernels, local(): pl.pallas_call(add_cut_terms, out_shape=jax.ShapeDtypeStruct((NVAR, MODES...  1.88 us

profile of v3, /device:TPU:1, one launch (start us, length us, event | category | flops | bytes accessed | tf_op | source)
XLA Modules:
  0.0 34.1 jit_solution(4138434373178017003)
XLA Ops:
  0.0 32.2 %residual_step.1 = (f32[5,125,1024]{2,1,0:T(8,128)S(1)}, f32[10,32,128]{2,1,0:T(8,128)S(1)}, bf16[64,1024]{1,0:T(8,128)(2,1)S(1)}) custom-call(f32[5,125,1024]{2,1,0:T(8,128)} %state_hbm.1, f32[5,125,1024]{2,1,0:T(8,128)} %old_hbm.1, f32[125,40,125]{2,1,0:T(8,128)} %bitcast.6, f32[125,40,125]{2,1,0:T(8,128)} %bitcast.7, f32[1,1024]{1,0:T(1,128)} %bitcast.9, ...), custom_call_target="tpu_custom_call" | custom-call | tf_op jit(solution)/shard_map/residual_step/pallas_call | solution.py:631
  32.2 1.9 %add_cut_terms.1 = f32[5,125,1024]{2,1,0:T(8,128)} custom-call(f32[5,125,1024]{2,1,0:T(8,128)S(1)} %get-tuple-element.8.part, f32[10,32,128]{2,1,0:T(8,128)S(1)} %get-tuple-element.9.got, bf16[64,1024]{1,0:T(8,128)(2,1)S(1)} %get-tuple-element.10.asked_rows), custom_call_target="tpu_custom_call" | custom-call | tf_op jit(solution)/shard_map/add_cut_terms/pallas_call | solution.py:703

commit v4 on v3

--- a/solution.py
+++ b/solution.py
@@ -158,8 +158,17 @@
         return carry
 
     lax.fori_loop(1, PEERS, greet, 0)
-    for neighbour in (above, below):
-        pl.semaphore_signal(barrier, inc=1, device_id={"px": neighbour}, device_id_type=MESH)
+    has_above = pz < npx - 1
+    has_below = pz > 0
+
+    @pl.when(has_above)
+    def _():
+        pl.semaphore_signal(barrier, inc=1, device_id={"px": above}, device_id_type=MESH)
+
+    @pl.when(has_below)
+    def _():
+        pl.semaphore_signal(barrier, inc=1, device_id={"px": below}, device_id_type=MESH)
+
 
     load_state = pltpu.make_async_copy(state_hbm, st, load_sem.at[0])
     load_old = pltpu.make_async_copy(old_hbm, so, load_sem.at[1])
@@ -262,7 +271,8 @@
 
     lax.fori_loop(0, NVAR, build, 0)
 
-    pl.semaphore_wait(barrier, PEERS + 1)
+    nearby = jnp.where(has_above, 1, 0) + jnp.where(has_below, 1, 0)
+    pl.semaphore_wait(barrier, PEERS - 1 + nearby)
 
     def id_copy(r):
         return pltpu.make_async_remote_copy(
@@ -332,8 +342,15 @@
         device_id={"px": above},
         device_id_type=MESH,
     )
-    rim_down.start()
-    rim_up.start()
+
+    @pl.when(has_below)
+    def _():
+        rim_down.start()
+
+    @pl.when(has_above)
+    def _():
+        rim_up.start()
+
 
     body1.wait_recv()
     bsum1[...] = bown[...] + bgot1[...]
@@ -429,12 +446,21 @@
         )
         body3[-1].start()
 
-    rim_down.wait_recv()
-    rim_up.wait_recv()
-    rim = trx[:, 32:64, 1152:1280]
-    trx[:, 32:64, 1152:1280] = jnp.where(pz == npx - 1, 0.0, rim)
-    rim = trx[:, 0:32, 0:128]
-    trx[:, 0:32, 0:128] = jnp.where(pz == 0, 0.0, rim)
+    @pl.when(has_above)
+    def _():
+        rim_down.wait_recv()
+
+    @pl.when(jnp.logical_not(has_above))
+    def _():
+        trx[:, 32:64, 1152:1280] = jnp.zeros((NVAR, 32, 128), F32)
+
+    @pl.when(has_below)
+    def _():
+        rim_up.wait_recv()
+
+    @pl.when(jnp.logical_not(has_below))
+    def _():
+        trx[:, 0:32, 0:128] = jnp.zeros((NVAR, 32, 128), F32)
 
     mi, mrest = divmod_const(iota((MODES, 256), 0), 25)
     mj = jnp.floor((mrest + 0.5) * 0.2)
@@ -564,8 +590,15 @@
     body1.wait_send()
     for copy in body2 + body3:
         copy.wait_send()
-    rim_down.wait_send()
-    rim_up.wait_send()
+
+    @pl.when(has_below)
+    def _():
+        rim_down.wait_send()
+
+    @pl.when(has_above)
+    def _():
+        rim_up.wait_send()
+
     asked_rows[...] = onehot[0:SLOTS, :]
 
     pltpu.make_async_copy(p3recv, p3recv, p3_recv).wait()

time: 34.2 us -> 30.7 us (0.90)
  Pallas kernels: 34.1 us -> 30.6 us
    pallas_call x1, Pallas kernels: 32.2 us -> 28.7 us  [local(): pl.pallas_call(kernel, out_shape=(pltpu.VMEM((NVAR, MODES, ELEM), F32), p...]
where the time goes in v4:
time: 30.7 us; the launch traced here: 30.6 us
  Pallas kernels  30.6 us (100%)
    pallas_call x1, Pallas kernels, local(): pl.pallas_call(kernel, out_shape=(pltpu.VMEM((NVAR, MODES, ELEM), F32), p...  28.7 us
    pallas_call x1, Pallas kernels, local(): pl.pallas_call(add_cut_terms, out_shape=jax.ShapeDtypeStruct((NVAR, MODES...  1.88 us

profile of v4, /device:TPU:1, one launch (start us, length us, event | category | flops | bytes accessed | tf_op | source)
XLA Modules:
  0.0 30.6 jit_solution(1543202932693546041)
XLA Ops:
  0.0 28.7 %residual_step.1 = (f32[5,125,1024]{2,1,0:T(8,128)S(1)}, f32[10,32,128]{2,1,0:T(8,128)S(1)}, bf16[64,1024]{1,0:T(8,128)(2,1)S(1)}) custom-call(f32[5,125,1024]{2,1,0:T(8,128)} %state_hbm.1, f32[5,125,1024]{2,1,0:T(8,128)} %old_hbm.1, f32[125,40,125]{2,1,0:T(8,128)} %bitcast.6, f32[125,40,125]{2,1,0:T(8,128)} %bitcast.7, f32[1,1024]{1,0:T(1,128)} %bitcast.9, ...), custom_call_target="tpu_custom_call" | custom-call | tf_op jit(solution)/shard_map/residual_step/pallas_call | solution.py:664
  28.7 1.9 %add_cut_terms.1 = f32[5,125,1024]{2,1,0:T(8,128)} custom-call(f32[5,125,1024]{2,1,0:T(8,128)S(1)} %get-tuple-element.8.part, f32[10,32,128]{2,1,0:T(8,128)S(1)} %get-tuple-element.9.got, bf16[64,1024]{1,0:T(8,128)(2,1)S(1)} %get-tuple-element.10.asked_rows), custom_call_target="tpu_custom_call" | custom-call | tf_op jit(solution)/shard_map/add_cut_terms/pallas_call | solution.py:736

commit v5 on v4

--- a/solution.py
+++ b/solution.py
@@ -103,7 +103,7 @@
     so,
     mats,
     uhl,
-    chl,
+    across,
     vpad,
     mhh,
     mlo,
@@ -288,7 +288,7 @@
         id_copy(r).start()
         return carry
 
-    lax.fori_loop(1, PEERS, id_start, 0)
+    lax.fori_loop(1, PEERS, id_start, 0, unroll=True)
     pltpu.make_async_copy(ids_row, ids_all.at[pl.ds(me, 1), :], id_recv).start()
 
     core = lax.rem(me, 2)
@@ -315,14 +315,17 @@
         tcols = pl.ds(pl.multiple_of(j * 256 + 128, 128), 256)
         for v in range(NVAR):
             rows = pl.ds(v * PAD, PAD)
-            u = st[v, :, cols]
-            high, low = split(pad_rows(u))
+            u = pad_rows(st[v, :, cols])
+            high, low = split(u)
             uhl[0, rows, cols] = high
             uhl[1, rows, cols] = low
             trx[v, :, tcols] = dot(trace_op, high) + dot(trace_op, low)
-            high, low = split(pad_rows(u - so[v, :, cols]))
-            chl[0, rows, cols] = high
-            chl[1, rows, cols] = low
+            high, low = split(u.T)
+            across[0, cols, rows] = high
+            across[1, cols, rows] = low
+            high, low = split((u - pad_rows(so[v, :, cols])).T)
+            across[2, cols, rows] = high
+            across[3, cols, rows] = low
         return carry
 
     lax.fori_loop(0, 4, split_state, 0)
@@ -368,26 +371,6 @@
         )
         body2[-1].start()
 
-    load_mass.wait()
-    load_oper.wait()
-
-    def split_cut(i, carry):
-        rows = pl.ds(pl.multiple_of(i * (8 * CUTS), 8 * CUTS), 8 * CUTS)
-        for t in range(2):
-            high, low = split(pad_lanes(mats[t, pl.ds(i * 8, 8)].reshape(8 * CUTS, MODES)))
-            cuth[rows, t * PAD : (t + 1) * PAD] = high
-            cutl[rows, t * PAD : (t + 1) * PAD] = low
-        return carry
-
-    lax.fori_loop(0, MODES // 8, split_cut, 0)
-    whole = MODES // 8 * 8
-    for t in range(2):
-        tail = pad_lanes(mats[t, whole:MODES].reshape((MODES - whole) * CUTS, MODES))
-        zero = jnp.zeros(((PAD - MODES) * CUTS, PAD), F32)
-        high, low = split(jnp.concatenate([tail, zero], axis=0))
-        cuth[whole * CUTS :, t * PAD : (t + 1) * PAD] = high
-        cutl[whole * CUTS :, t * PAD : (t + 1) * PAD] = low
-
     pltpu.make_async_copy(ids_all, ids_all, id_recv).wait()
     asked = ids_all[...]
     lane = iota((PEERS, 128), 1)
@@ -396,10 +379,11 @@
         wanted = jnp.sum(jnp.where(lane == me + k * PEERS, asked, 0), axis=1, keepdims=True)
         rows = slice(k * PEERS, (k + 1) * PEERS)
         onehot[rows, :] = jnp.where(wanted == elem_lane, 1.0, 0.0).astype(BF16)
-    state_high = dot_nt(onehot[...], uhl[0])
-    state_low = dot_nt(onehot[...], uhl[1])
+    state_high = dot(onehot[...], across[0])
+    state_low = dot(onehot[...], across[1])
     state_cols = state_high + state_low
-    change_cols = dot_nt(onehot[0:SLOTS, :], chl[0]) + dot_nt(onehot[0:SLOTS, :], chl[1])
+    asking = onehot[0:SLOTS, :]
+    change_cols = dot(asking, across[2]) + dot(asking, across[3])
     for k in range(2):
         rows = slice(k * PEERS, (k + 1) * PEERS)
         for v in range(NVAR):
@@ -424,27 +408,10 @@
         p2_copy(r).start()
         return carry
 
-    lax.fori_loop(1, PEERS, p2_start, 0)
+    lax.fori_loop(1, PEERS, p2_start, 0, unroll=True)
     pltpu.make_async_copy(
         p2send.at[:, pl.ds(me, 1), :], p2recv.at[:, pl.ds(me, 1), :], p2_recv
     ).start()
-
-    for copy in body2:
-        copy.wait_recv()
-    bsum2[...] = bsum1[...] + bgot2[0] + bgot2[1] + bgot2[2]
-    body3 = []
-    for r in range(1, 4):
-        body3.append(
-            pltpu.make_async_remote_copy(
-                src_ref=bsum2,
-                dst_ref=bgot3.at[r - 1],
-                send_sem=b_send.at[3 + r],
-                recv_sem=b_recv.at[3 + r],
-                device_id={"py": lax.rem(py_in + r, 4) * 8 + px_in * 2 + core},
-                device_id_type=MESH,
-            )
-        )
-        body3[-1].start()
 
     @pl.when(has_above)
     def _():
@@ -489,6 +456,43 @@
 
     lax.fori_loop(0, 4, volume, 0)
 
+    for copy in body2:
+        copy.wait_recv()
+    bsum2[...] = bsum1[...] + bgot2[0] + bgot2[1] + bgot2[2]
+    body3 = []
+    for r in range(1, 4):
+        body3.append(
+            pltpu.make_async_remote_copy(
+                src_ref=bsum2,
+                dst_ref=bgot3.at[r - 1],
+                send_sem=b_send.at[3 + r],
+                recv_sem=b_recv.at[3 + r],
+                device_id={"py": lax.rem(py_in + r, 4) * 8 + px_in * 2 + core},
+                device_id_type=MESH,
+            )
+        )
+        body3[-1].start()
+
+    load_mass.wait()
+    load_oper.wait()
+
+    def split_cut(i, carry):
+        rows = pl.ds(pl.multiple_of(i * (8 * CUTS), 8 * CUTS), 8 * CUTS)
+        for t in range(2):
+            high, low = split(pad_lanes(mats[t, pl.ds(i * 8, 8)].reshape(8 * CUTS, MODES)))
+            cuth[rows, t * PAD : (t + 1) * PAD] = high
+            cutl[rows, t * PAD : (t + 1) * PAD] = low
+        return carry
+
+    lax.fori_loop(0, MODES // 8, split_cut, 0)
+    whole = MODES // 8 * 8
+    for t in range(2):
+        tail = pad_lanes(mats[t, whole:MODES].reshape((MODES - whole) * CUTS, MODES))
+        zero = jnp.zeros(((PAD - MODES) * CUTS, PAD), F32)
+        high, low = split(jnp.concatenate([tail, zero], axis=0))
+        cuth[whole * CUTS :, t * PAD : (t + 1) * PAD] = high
+        cutl[whole * CUTS :, t * PAD : (t + 1) * PAD] = low
+
     pltpu.make_async_copy(p2recv, p2recv, p2_recv).wait()
     xh[...] = jnp.zeros_like(xh)
     xl[...] = jnp.zeros_like(xl)
@@ -531,7 +535,7 @@
         p3_copy(r).start()
         return carry
 
-    lax.fori_loop(1, PEERS, p3_start, 0)
+    lax.fori_loop(1, PEERS, p3_start, 0, unroll=True)
     pltpu.make_async_copy(
         p3send.at[:, pl.ds(me, 1), :], p3recv.at[:, pl.ds(me, 1), :], p3_recv
     ).start()
@@ -686,7 +690,7 @@
             pltpu.VMEM((NVAR, MODES, ELEM), F32),
             pltpu.VMEM((2, MODES, CUTS, MODES), F32),
             pltpu.VMEM((2, WIDTH, ELEM), BF16),
-            pltpu.VMEM((2, WIDTH, ELEM), BF16),
+            pltpu.VMEM((4, ELEM, WIDTH), BF16),
             pltpu.VMEM((3, PAD, PAD), F32),
             pltpu.VMEM((WIDTH, 2 * WIDTH), BF16),
             pltpu.VMEM((WIDTH, WIDTH), BF16),

time: 30.7 us -> 30.6 us (level); the launches traced: 30.6 us -> 30.2 us
  Pallas kernels: 30.6 us -> 30.1 us
    pallas_call x1, Pallas kernels: 28.7 us -> 28.3 us  [local(): pl.pallas_call(kernel, out_shape=(pltpu.VMEM((NVAR, MODES, ELEM), F32), p...]
where the time goes in v5:
time: 30.6 us; the launch traced here: 30.2 us
  Pallas kernels  30.1 us (98%)
    pallas_call x1, Pallas kernels, local(): pl.pallas_call(kernel, out_shape=(pltpu.VMEM((NVAR, MODES, ELEM), F32), p...  28.3 us
    pallas_call x1, Pallas kernels, local(): pl.pallas_call(add_cut_terms, out_shape=jax.ShapeDtypeStruct((NVAR, MODES...  1.88 us

profile of v5, /device:TPU:1, one launch (start us, length us, event | category | flops | bytes accessed | tf_op | source)
XLA Modules:
  0.0 30.2 jit_solution(13602268245724007655)
XLA Ops:
  0.0 28.3 %residual_step.1 = (f32[5,125,1024]{2,1,0:T(8,128)S(1)}, f32[10,32,128]{2,1,0:T(8,128)S(1)}, bf16[64,1024]{1,0:T(8,128)(2,1)S(1)}) custom-call(f32[5,125,1024]{2,1,0:T(8,128)} %state_hbm.1, f32[5,125,1024]{2,1,0:T(8,128)} %old_hbm.1, f32[125,40,125]{2,1,0:T(8,128)} %bitcast.6, f32[125,40,125]{2,1,0:T(8,128)} %bitcast.7, f32[1,1024]{1,0:T(1,128)} %bitcast.9, ...), custom_call_target="tpu_custom_call" | custom-call | tf_op jit(solution)/shard_map/residual_step/pallas_call | solution.py:668
  28.3 1.9 %add_cut_terms.1 = f32[5,125,1024]{2,1,0:T(8,128)} custom-call(f32[5,125,1024]{2,1,0:T(8,128)S(1)} %get-tuple-element.8.part, f32[10,32,128]{2,1,0:T(8,128)S(1)} %get-tuple-element.9.got, bf16[64,1024]{1,0:T(8,128)(2,1)S(1)} %get-tuple-element.10.asked_rows), custom_call_target="tpu_custom_call" | custom-call | tf_op jit(solution)/shard_map/add_cut_terms/pallas_call | solution.py:740

commit v6 on v5

--- a/solution.py
+++ b/solution.py
@@ -413,22 +413,6 @@
         p2send.at[:, pl.ds(me, 1), :], p2recv.at[:, pl.ds(me, 1), :], p2_recv
     ).start()
 
-    @pl.when(has_above)
-    def _():
-        rim_down.wait_recv()
-
-    @pl.when(jnp.logical_not(has_above))
-    def _():
-        trx[:, 32:64, 1152:1280] = jnp.zeros((NVAR, 32, 128), F32)
-
-    @pl.when(has_below)
-    def _():
-        rim_up.wait_recv()
-
-    @pl.when(jnp.logical_not(has_below))
-    def _():
-        trx[:, 0:32, 0:128] = jnp.zeros((NVAR, 32, 128), F32)
-
     mi, mrest = divmod_const(iota((MODES, 256), 0), 25)
     mj = jnp.floor((mrest + 0.5) * 0.2)
     mk = mrest - mj * 5.0
@@ -442,16 +426,8 @@
         )
         scale = mode_weight * jac[:, cols]
         for v in range(NVAR):
-            near = jnp.concatenate(
-                [trx[v, 0:32, cols], trx[v, 32:64, pl.ds(pl.multiple_of(base + 256, 256), 256)]],
-                axis=0,
-            )
-            high, low = split(near)
-            faces = dot(expand_op, jnp.concatenate([high, low], axis=0))
             change = st[v, :, cols] - so[v, :, cols]
-            part[v, :, cols] = (
-                acc[v * PAD : v * PAD + MODES] + scale * change - penalty[v] * faces[0:MODES]
-            )
+            part[v, :, cols] = acc[v * PAD : v * PAD + MODES] + scale * change
         return carry
 
     lax.fori_loop(0, 4, volume, 0)
@@ -539,6 +515,37 @@
     pltpu.make_async_copy(
         p3send.at[:, pl.ds(me, 1), :], p3recv.at[:, pl.ds(me, 1), :], p3_recv
     ).start()
+
+    @pl.when(has_above)
+    def _():
+        rim_down.wait_recv()
+
+    @pl.when(jnp.logical_not(has_above))
+    def _():
+        trx[:, 32:64, 1152:1280] = jnp.zeros((NVAR, 32, 128), F32)
+
+    @pl.when(has_below)
+    def _():
+        rim_up.wait_recv()
+
+    @pl.when(jnp.logical_not(has_below))
+    def _():
+        trx[:, 0:32, 0:128] = jnp.zeros((NVAR, 32, 128), F32)
+
+    def neighbours(j, carry):
+        base = pl.multiple_of(j * 256, 256)
+        cols = pl.ds(base, 256)
+        for v in range(NVAR):
+            near = jnp.concatenate(
+                [trx[v, 0:32, cols], trx[v, 32:64, pl.ds(pl.multiple_of(base + 256, 256), 256)]],
+                axis=0,
+            )
+            high, low = split(near)
+            faces = dot(expand_op, jnp.concatenate([high, low], axis=0))
+            part[v, :, cols] = part[v, :, cols] - penalty[v] * faces[0:MODES]
+        return carry
+
+    lax.fori_loop(0, 4, neighbours, 0)
 
     for copy in body3:
         copy.wait_recv()

time: 30.6 us -> 30.1 us (0.984)
  no operation moved by 1% of the time
where the time goes in v6:
time: 30.1 us; the launch traced here: 29.9 us
  Pallas kernels  29.9 us (99%)
    pallas_call x1, Pallas kernels, local(): pl.pallas_call(kernel, out_shape=(pltpu.VMEM((NVAR, MODES, ELEM), F32), p...  28 us
    pallas_call x1, Pallas kernels, local(): pl.pallas_call(add_cut_terms, out_shape=jax.ShapeDtypeStruct((NVAR, MODES...  1.88 us

profile of v6, /device:TPU:1, one launch (start us, length us, event | category | flops | bytes accessed | tf_op | source)
XLA Modules:
  0.0 29.9 jit_solution(1481618726676444594)
XLA Ops:
  0.0 28.0 %residual_step.1 = (f32[5,125,1024]{2,1,0:T(8,128)S(1)}, f32[10,32,128]{2,1,0:T(8,128)S(1)}, bf16[64,1024]{1,0:T(8,128)(2,1)S(1)}) custom-call(f32[5,125,1024]{2,1,0:T(8,128)} %state_hbm.1, f32[5,125,1024]{2,1,0:T(8,128)} %old_hbm.1, f32[125,40,125]{2,1,0:T(8,128)} %bitcast.6, f32[125,40,125]{2,1,0:T(8,128)} %bitcast.7, f32[1,1024]{1,0:T(1,128)} %bitcast.9, ...), custom_call_target="tpu_custom_call" | custom-call | tf_op jit(solution)/shard_map/residual_step/pallas_call | solution.py:675
  28.0 1.9 %add_cut_terms.1 = f32[5,125,1024]{2,1,0:T(8,128)} custom-call(f32[5,125,1024]{2,1,0:T(8,128)S(1)} %get-tuple-element.8.part, f32[10,32,128]{2,1,0:T(8,128)S(1)} %get-tuple-element.9.got, bf16[64,1024]{1,0:T(8,128)(2,1)S(1)} %get-tuple-element.10.asked_rows), custom_call_target="tpu_custom_call" | custom-call | tf_op jit(solution)/shard_map/add_cut_terms/pallas_call | solution.py:747

commit v7 on v6

--- a/solution.py
+++ b/solution.py
@@ -151,24 +151,24 @@
     above = lax.rem(pz + 1, npx)
     below = lax.rem(pz + npx - 1, npx)
 
+    has_above = pz < npx - 1
+    has_below = pz > 0
+
+    @pl.when(has_above)
+    def _():
+        pl.semaphore_signal(barrier, inc=1, device_id={"px": above}, device_id_type=MESH)
+
+    @pl.when(has_below)
+    def _():
+        pl.semaphore_signal(barrier, inc=1, device_id={"px": below}, device_id_type=MESH)
+
     def greet(r, carry):
         pl.semaphore_signal(
             barrier, inc=1, device_id={"py": lax.rem(me + r, PEERS)}, device_id_type=MESH
         )
         return carry
 
-    lax.fori_loop(1, PEERS, greet, 0)
-    has_above = pz < npx - 1
-    has_below = pz > 0
-
-    @pl.when(has_above)
-    def _():
-        pl.semaphore_signal(barrier, inc=1, device_id={"px": above}, device_id_type=MESH)
-
-    @pl.when(has_below)
-    def _():
-        pl.semaphore_signal(barrier, inc=1, device_id={"px": below}, device_id_type=MESH)
-
+    lax.fori_loop(1, PEERS, greet, 0, unroll=True)
 
     load_state = pltpu.make_async_copy(state_hbm, st, load_sem.at[0])
     load_old = pltpu.make_async_copy(old_hbm, so, load_sem.at[1])
@@ -619,7 +619,7 @@
         p3_copy(r).wait_send()
         return carry
 
-    lax.fori_loop(1, PEERS, left, 0)
+    lax.fori_loop(1, PEERS, left, 0, unroll=True)
 
 
 def add_cut_terms(part, got, asked_rows, out_hbm, total, out_sem):

time: 30.1 us -> 29.8 us (0.990)
  no operation moved by 1% of the time
where the time goes in v7:
time: 29.8 us; the launch traced here: 29.7 us
  Pallas kernels  29.7 us (100%)
    pallas_call x1, Pallas kernels, local(): pl.pallas_call(kernel, out_shape=(pltpu.VMEM((NVAR, MODES, ELEM), F32), p...  27.8 us
    pallas_call x1, Pallas kernels, local(): pl.pallas_call(add_cut_terms, out_shape=jax.ShapeDtypeStruct((NVAR, MODES...  1.88 us

profile of v7, /device:TPU:1, one launch (start us, length us, event | category | flops | bytes accessed | tf_op | source)
XLA Modules:
  0.0 29.7 jit_solution(5605483505117961246)
XLA Ops:
  0.0 27.8 %residual_step.1 = (f32[5,125,1024]{2,1,0:T(8,128)S(1)}, f32[10,32,128]{2,1,0:T(8,128)S(1)}, bf16[64,1024]{1,0:T(8,128)(2,1)S(1)}) custom-call(f32[5,125,1024]{2,1,0:T(8,128)} %state_hbm.1, f32[5,125,1024]{2,1,0:T(8,128)} %old_hbm.1, f32[125,40,125]{2,1,0:T(8,128)} %bitcast.6, f32[125,40,125]{2,1,0:T(8,128)} %bitcast.7, f32[1,1024]{1,0:T(1,128)} %bitcast.9, ...), custom_call_target="tpu_custom_call" | custom-call | tf_op jit(solution)/shard_map/residual_step/pallas_call | solution.py:675
  27.8 1.9 %add_cut_terms.1 = f32[5,125,1024]{2,1,0:T(8,128)} custom-call(f32[5,125,1024]{2,1,0:T(8,128)S(1)} %get-tuple-element.8.part, f32[10,32,128]{2,1,0:T(8,128)S(1)} %get-tuple-element.9.got, bf16[64,1024]{1,0:T(8,128)(2,1)S(1)} %get-tuple-element.10.asked_rows), custom_call_target="tpu_custom_call" | custom-call | tf_op jit(solution)/shard_map/add_cut_terms/pallas_call | solution.py:747
